TPU v7x, 256 devices: a whole 4x4x8 slice. The times are simulated.
256 devices in a mesh: ctx: 32 (over y, z), head: 8 (over x, core).
Axes of the slice: x: 4, y: 4, z: 8, core: 2. Of those that a mesh axis runs over, the one named last changes fastest.
Arguments:
- queries: bfloat16 [32768, 128], P('ctx'), may hold values from -2 to 2
- keys: bfloat16 [32768, 128], P('ctx'), may hold values from -2 to 2
- values: bfloat16 [32768, 2048], P('ctx', 'head'), may hold values from -6 to 6
- gates: float32 [16, 32768], P('head', 'ctx'), may hold values from -2.5 to 0
- level_weights: float32 [16, 10, 32768], P('head', None, 'ctx'), may hold values from 0 to 4
- segment: int32 [32768], P('ctx'), may hold values from 0 to 7, never falling along the last dimension, each value on 1 to 16384 neighbouring positions
- cotangent: bfloat16 [32768, 2048], P('ctx', 'head'), may hold values from -0.59765625 to 0.59765625
Outputs:
- query_grad: float32 [32768, 128], P(('ctx', 'head'))
- key_grad: float32 [32768, 128], P(('ctx', 'head'))
- value_grad: float32 [32768, 2048], P('ctx', 'head')
- gate_grad: float32 [16, 32768], P('head', 'ctx')
- weight_grad: float32 [16, 10, 32768], P('head', None, 'ctx')
Inputs may be any that keep to these rules, and one draw needn't show every extreme that they name: `segment`: document numbers never fall along the tokens; every number is used, each document holds 1 to 16384 tokens and one holds exactly that many.
All inputs are finite; a program needn't handle non-finite values.
Results may differ from a plain program's by a relative error of at most 0.0003.
Values sent between devices are 32-bit elements; how exact they have to be, the bound alone decides.
A program may use at most 64 MiB of HBM per device.

v0:
```python
import jax
import jax.numpy as jnp
from jax import lax
from jax.sharding import PartitionSpec as P

STRETCH = 128


PRECISE = lax.Precision.HIGHEST


def entering(x, axis, combine, identity):
    length, index = (lax.axis_size(axis), lax.axis_index(axis))
    everything = lax.all_gather(x, axis)
    start = jnp.broadcast_to(jnp.asarray(identity, x.dtype), x.shape)

    def turn(k, before):
        at = length - 1 - k
        reached = at > index
        new = combine(before, everything[at])
        return jnp.where(reached, new, before)

    return lax.fori_loop(0, length, turn, start)


def stretch_tables(gates, segment):
    num_stretches = segment.shape[0] // STRETCH
    seg_stretches = segment.reshape(num_stretches, STRETCH)
    within = jnp.cumsum(gates.reshape(num_stretches, STRETCH), axis=1)
    stretch_total = within[:, -1]
    return (seg_stretches, within, stretch_total, jnp.cumsum(stretch_total), seg_stretches[:, -1])


def stretch_mix(
    query_stretches, key_stretches, value_stretches, seg_stretches, within, first_weight
):
    offsets = jnp.arange(STRETCH)
    causal = offsets[:, None] >= offsets[None, :]
    allowed = causal[None] & (seg_stretches[:, :, None] == seg_stretches[:, None, :])
    decays = jnp.where(
        allowed, jnp.exp(jnp.minimum(within[:, :, None] - within[:, None, :], 0.0)), 0.0
    )
    scores = jnp.einsum("cti,csi->cts", query_stretches, key_stretches, precision=PRECISE)
    return jnp.einsum(
        "cts,csj->ctj",
        first_weight[:, :, None] * decays * scores,
        value_stretches,
        precision=PRECISE,
    )


def merge_blocks(blocks, block_span, stretch_cum, seg_end):
    num_blocks = blocks.shape[0]
    block_ends = jnp.arange(num_blocks) * block_span + block_span - 1
    lower_end = block_ends[0::2]
    upper_end = block_ends[1::2]
    linkage = jnp.where(
        seg_end[lower_end] == seg_end[upper_end],
        jnp.exp(jnp.minimum(stretch_cum[upper_end] - stretch_cum[lower_end], 0.0)),
        0.0,
    )
    return blocks[0::2] * linkage[:, None, None] + blocks[1::2]


def bridge(source_end, active, prior_stretch, stretch_cum, seg_end):
    source = jnp.maximum(source_end, 0)
    allowed = active & (seg_end[source] == seg_end[prior_stretch])
    return jnp.where(
        allowed, jnp.exp(jnp.minimum(stretch_cum[prior_stretch] - stretch_cum[source], 0.0)), 0.0
    )


def half_level(queries, blocks, block_span, token_weight):
    num_stretches = token_weight.shape[0]
    num_pairs = num_stretches // (2 * block_span)
    paired_weight = token_weight.reshape(num_pairs, 2, block_span * STRETCH)
    query_pairs = queries.reshape(num_pairs, 2, block_span * STRETCH, queries.shape[1])
    upper_out = jnp.einsum(
        "nti,nij->ntj",
        query_pairs[:, 1] * paired_weight[:, 1, :, None],
        blocks[0::2],
        precision=PRECISE,
    )
    return jnp.stack([jnp.zeros_like(upper_out), upper_out], axis=1).reshape(
        num_stretches * STRETCH, upper_out.shape[2]
    )


def states_head(keys, values, gates, segment):
    num_stretches = segment.shape[0] // STRETCH
    seg_stretches, within, stretch_total, stretch_cum, seg_end = stretch_tables(gates, segment)
    key_weight = jnp.where(
        seg_stretches == seg_end[:, None], jnp.exp(stretch_total[:, None] - within), 0.0
    )
    blocks = jnp.einsum(
        "csi,csj->cij",
        keys.reshape(num_stretches, STRETCH, -1) * key_weight[:, :, None],
        values.reshape(num_stretches, STRETCH, -1),
        precision=PRECISE,
    )
    stacked = [blocks]
    block_span = 1
    for step_num in range(num_stretches.bit_length() - 1):
        blocks = merge_blocks(blocks, block_span, stretch_cum, seg_end)
        stacked.append(blocks)
        block_span = 2 * block_span
    return stacked


def outputs_head(queries, keys, values, weights, level_blocks, remote, gates, segment, prev_end):
    length = queries.shape[0]
    num_stretches = length // STRETCH
    seg_stretches, within, stretch_total, stretch_cum, seg_end = stretch_tables(gates, segment)
    weight_stretches = weights.reshape(weights.shape[0], num_stretches, STRETCH)
    summed = stretch_mix(
        queries.reshape(num_stretches, STRETCH, -1),
        keys.reshape(num_stretches, STRETCH, -1),
        values.reshape(num_stretches, STRETCH, -1),
        seg_stretches,
        within,
        weight_stretches[0],
    ).reshape(length, -1)
    prior_end = jnp.concatenate([jnp.full((1,), -1, jnp.int32), seg_end[:-1]])
    query_weight = jnp.where(seg_stretches == prior_end[:, None], jnp.exp(within), 0.0)
    stretch_idx = jnp.arange(num_stretches)
    prior_stretch = jnp.maximum(stretch_idx - 1, 0)
    block_span = 1
    for level_idx, blocks in enumerate(level_blocks):
        active = stretch_idx // block_span % 2 == 1
        linkage = bridge(
            stretch_idx // block_span * block_span - 1, active, prior_stretch, stretch_cum, seg_end
        )
        summed = summed + half_level(
            queries,
            blocks,
            block_span,
            linkage[:, None] * query_weight * weight_stretches[level_idx + 1],
        )
        block_span = 2 * block_span
    tree_depth = remote.shape[0]
    level_list = [
        min(len(level_blocks) + step_num, weights.shape[0] - 1)
        for step_num in range(1, tree_depth + 1)
    ]
    entry_weight = jnp.where(segment == prev_end, jnp.exp(jnp.cumsum(gates)), 0.0)
    scaled = jnp.stack([weights[row_num] * entry_weight for row_num in level_list], axis=1)
    spread_q = (scaled[:, :, None] * queries[:, None, :]).reshape(
        length, tree_depth * queries.shape[1]
    )
    return summed + jnp.dot(
        spread_q, remote.reshape(tree_depth * remote.shape[1], remote.shape[2]), precision=PRECISE
    )


def shards(queries, keys, values, gates, level_weights, segment, cotangent):
    num_heads = gates.shape[0]
    num_rows = queries.shape[0]
    head_width = values.shape[1] // num_heads
    shard_count = lax.axis_size("ctx")
    tree_depth = shard_count.bit_length() - 1
    position = lax.axis_index("ctx")
    query_full = queries.astype(jnp.float32)
    key_full = keys.astype(jnp.float32)
    query_heads = jnp.broadcast_to(query_full, (num_heads,) + query_full.shape)
    key_heads = jnp.broadcast_to(key_full, (num_heads,) + key_full.shape)
    value_heads = (
        values.astype(jnp.float32).reshape(num_rows, num_heads, head_width).transpose(1, 0, 2)
    )
    cotan_heads = (
        cotangent.astype(jnp.float32).reshape(num_rows, num_heads, head_width).transpose(1, 0, 2)
    )

    def states_all(key_in, value_in):
        return jax.vmap(states_head, in_axes=(0, 0, 0, None))(key_in, value_in, gates, segment)

    stacked, pull_states = jax.vjp(states_all, key_heads, value_heads)
    device_state = stacked[-1][:, 0]
    totals_all, last_segments = (
        lax.all_gather(jnp.sum(gates, axis=1)[None, :], "ctx", axis=0, tiled=True),
        lax.all_gather(segment[-1:].astype(jnp.float32), "ctx", axis=0, tiled=True),
    )
    running_sum = jnp.cumsum(totals_all, axis=0)
    end_numbers = last_segments.astype(jnp.int32)
    prev_end = end_numbers[jnp.maximum(position - 1, 0)]

    def between(first_dev, last_dev):
        same_doc = jnp.expand_dims(end_numbers[first_dev] == end_numbers[last_dev], -1)
        return jnp.where(
            same_doc, jnp.exp(jnp.minimum(running_sum[last_dev] - running_sum[first_dev], 0.0)), 0.0
        )

    device_idx = jnp.arange(shard_count)
    linkage = between(device_idx, jnp.maximum(position - 1, 0))
    level_masks = []
    uppers = []
    leads = []
    throughs = []
    for bit_num in range(tree_depth):
        block_span = 2**bit_num
        is_upper = position // block_span % 2 == 1
        same_group = device_idx // (2 * block_span) == position // (2 * block_span)
        level_masks.append(same_group & is_upper & (device_idx // block_span % 2 == 0))
        block_start = position // block_span * block_span
        leads.append(between(jnp.maximum(block_start - 1, 0), jnp.maximum(position - 1, 0)))
        upper_start = position // (2 * block_span) * (2 * block_span) + block_span
        throughs.append(between(upper_start - 1, upper_start + block_span - 1))
        uppers.append(is_upper)
    level_table = jnp.where(jnp.stack(level_masks)[:, :, None], linkage[None], 0.0)
    shard_rows = jax.tree.map(
        lambda part: lax.all_gather(part, "ctx", axis=0, tiled=True), device_state[None]
    )
    window = lax.slice_in_dim(level_table, 0, shard_rows.shape[0], axis=1)
    remote = jnp.zeros((tree_depth,) + device_state.shape, jnp.float32) + jnp.einsum(
        "mnh,nhij->mhij", window, shard_rows, precision=PRECISE
    )

    def outputs_all(query_in, key_in, value_in, weight_in, blocks_in, remote_in):
        return jax.vmap(outputs_head, in_axes=(0, 0, 0, 0, 0, 1, 0, None, None))(
            query_in, key_in, value_in, weight_in, blocks_in, remote_in, gates, segment, prev_end
        )

    _, pull_outputs = jax.vjp(
        outputs_all, query_heads, key_heads, value_heads, level_weights, stacked[:-1], remote
    )
    query_part, key_part, value_part, weight_grad, block_grads, remote_grad = pull_outputs(
        cotan_heads
    )
    window = level_table
    state_grad = lax.psum_scatter(
        jnp.einsum("mnh,mhij->nhij", window, remote_grad, precision=PRECISE),
        "ctx",
        scatter_dimension=0,
        tiled=True,
    )[0]
    key_state, value_state = pull_states(list(block_grads) + [state_grad[:, None]])
    key_total = key_part + key_state
    value_total = value_part + value_state
    gate_terms = jnp.einsum("ti,hti->ht", query_full, query_part, precision=PRECISE) - jnp.einsum(
        "ti,hti->ht", key_full, key_total, precision=PRECISE
    )
    suffix = jnp.flip(jnp.cumsum(jnp.flip(gate_terms, 1), axis=1), 1)
    later_sum = entering(suffix[:, 0], "ctx", jnp.add, jnp.zeros_like(suffix[:, 0]))
    gate_grad = suffix + later_sum[:, None]
    query_grad, key_grad = (
        lax.psum_scatter(jnp.sum(query_part, axis=0), "head", scatter_dimension=0, tiled=True),
        lax.psum_scatter(jnp.sum(key_total, axis=0), "head", scatter_dimension=0, tiled=True),
    )
    value_grad = value_total.transpose(1, 0, 2).reshape(num_rows, num_heads * head_width)
    return (query_grad, key_grad, value_grad, gate_grad, weight_grad)


def solution(mesh):
    return jax.shard_map(
        shards,
        mesh=mesh,
        in_specs=(
            P("ctx", None),
            P("ctx", None),
            P("ctx", "head"),
            P("head", "ctx"),
            P("head", None, "ctx"),
            P("ctx"),
            P("ctx", "head"),
        ),
        out_specs=(
            P(("ctx", "head"), None),
            P(("ctx", "head"), None),
            P("ctx", "head"),
            P("head", "ctx"),
            P("head", None, "ctx"),
        ),
        check_vma=False,
    )
```

profile of v0, /device:TPU:1, one launch (start us, length us, event | category | flops | bytes accessed | tf_op | source)
XLA Modules:
  0.0 559.2 jit_solution(10432785170736798503)
XLA Ops:
  7.2 0.9 slice_reduce_fusion.2
  8.1 0.9 fusion.117
  9.0 0.8 reduce_sum.90
  9.8 1.3 dynamic-slice.16
  11.7 1.5 convert_dynamic-update-slice_fusion
  13.4 64.6 %all-reduce.27 = (f32[64]{0:T(128)S(1)}, f32[32]{0:T(128)S(1)}) all-reduce(f32[64]{0:T(128)S(1)} %dynamic-update-slice.5, f32[32]{0:T(128)S(1)} %convert_dynamic-update-slice_fusion), channel_id=2, replica_groups=mesh['ctx'=32,'head'=8] {'ctx'}, use_global_device_ids=true, to_apply=%add.25 | all-reduce | flops 96 | bytes 768
  81.6 1.2 copy.181
  82.8 1.3 copy.202
  84.4 1.3 broadcast_compare_fusion
  86.4 1.3 broadcast_compare_fusion.3
  92.6 0.9 bitcast_multiply_fusion
  93.5 2.5 fusion.127
  96.0 3.5 fusion.11
  99.6 4.4 copy.275
  104.3 0.8 reshape.1329
  118.5 1.4 fusion.116
  128.3 1.0 bitcast_convert_fusion
  129.3 3.0 fusion.4
  132.3 195.9 %reduce-scatter.6.cloned.1.call-done = f32[1,2,128,128]{3,2,1,0:T(8,128)} async-done(((f32[32,2,128,128]{3,2,1,0:T(8,128)}), f32[1,2,128,128]{3,2,1,0:T(8,128)}) %reduce-scatter.6.cloned.1.call-update) | async-done | bytes 131088 | tf_op jit(solution)/shard_map/reduce_scatter | solution.py:229
  328.2 1.0 broadcast_multiply_fusion.2
  329.2 1.0 broadcast_multiply_fusion.1
  330.2 2.1 pad.84
  332.3 2.1 pad.83
  334.4 2.7 broadcast_multiply_fusion
  337.2 0.7 slice_add_fusion.1
  337.9 0.8 slice_add_fusion.2
  339.5 0.8 copy.237
  340.4 0.8 fusion.80
  341.2 1.8 multiply_reduce_fusion.4
  343.2 1.3 copy.213
  345.2 1.6 fusion.28
  346.7 5.7 %pad.78 = f32[2,8,128,128]{3,2,1,0:T(8,128)} pad(f32[2,4,128,128]{3,2,1,0:T(8,128)} %fusion.28, f32[]{:T(128)} %constant.358.clone.1), padding=0_0_0x0_1_1x0_0_0x0_0_0 | pad | bytes 1572868 | tf_op jit(solution)/shard_map/transpose(jvp(vmap()))/pad | solution.py:81
  353.3 2.3 fusion.30
  355.6 1.9 fusion.14
  357.6 2.2 multiply_reduce_fusion.3
  359.8 3.1 fusion.21
  362.9 1.8 multiply_reduce_fusion.5
  364.8 2.1 copy.248
  366.9 2.9 multiply_reduce_fusion.6
  369.7 2.0 copy.247
  371.8 5.7 %pad.86 = f32[2,8,128,128]{3,2,1,0:T(8,128)} pad(f32[2,4,128,128]{3,2,1,0:T(8,128)} %get-tuple-element.197, f32[]{:T(128)} %constant.358.clone.1), padding=0_0_0x0_1_1x0_0_0x0_0_0 | pad | bytes 1572868 | tf_op jit(solution)/shard_map/transpose(jvp(vmap()))/pad | solution.py:62
  377.5 5.8 %pad.85 = f32[2,8,128,128]{3,2,1,0:T(8,128)} pad(f32[2,4,128,128]{3,2,1,0:T(8,128)} %get-tuple-element.198, f32[]{:T(128)} %constant.358.clone.1), padding=0_0_0x1_0_1x0_0_0x0_0_0 | pad | bytes 1572868 | tf_op jit(solution)/shard_map/transpose(jvp(vmap()))/pad | solution.py:62
  383.2 3.5 fusion.6
  386.8 1.1 copy.276
  387.8 2.1 pad.76.clone
  389.9 2.6 copy.211
  392.5 2.2 pad.75.clone
  394.7 2.6 copy.209
  397.2 4.4 fusion.119
  401.6 19.2 %fusion.19 = f32[1024,1,2]{2,1,0:T(1,128)} fusion(f32[2,1024,128]{2,1,0:T(8,128)S(1)} %bitcast.312, bf16[1024,128,1]{1,0,2:T(8,128)(2,1)S(1)} %bitcast.318), kind=kOutput, calls=%fused_computation.49 | convolution fusion | flops 3145728 | bytes 1318912 | tf_op jit(solution)/shard_map/ti,hti->ht/dot_general | solution.py:238
  420.8 1.2 copy.236
  422.1 0.8 multiply_multiply_fusion.2
  423.8 6.8 %fusion = f32[2,5,128,128]{3,1,2,0:T(8,128)S(1)} fusion(f32[32,2,128,128]{3,2,1,0:T(8,128)} %bitcast.301, f32[32,2]{0,1:T(2,128)} %copy-done.34, pred[5,32]{1,0:T(8,128)(4,1)} %copy-done.35), kind=kOutput, calls=%fused_computation.22 | convolution fusion | flops 62914880 | bytes 4850080 | tf_op jit(solution)/shard_map/mnh,nhij->mhij/dot_general | solution.py:213
  430.8 2.2 fusion.126
  433.0 1.9 multiply_reduce_fusion
  434.9 2.6 copy.183
  437.5 6.1 %add_reduce_fusion = (f32[8,128,128]{2,1,0:T(8,128)}, f32[2,8,128,128]{3,2,1,0:T(8,128)}) fusion(f32[2,8,128,128]{3,2,1,0:T(8,128)S(1)} %bitcast.285, f32[2,8,128,128]{3,2,1,0:T(8,128)} %bitcast.287, f32[2,8,128,128]{3,2,1,0:T(8,128)} %bitcast.303, f32[2,8,128,128]{3,2,1,0:T(8,128)} %bitcast.289, f32[8,128,128]{2,1,0:T(8,128)S(1)} %bitcast_convert_fusion, ...), kind=kOutput, calls=%fused_computation.45 | convolution fusion | flops 405143552 | bytes 7487488 | tf_op jit(solution)/shard_map/transpose(jvp(vmap(cti,csi->cts)))/dot_general | solution.py:43
  443.6 1.6 copy.214
  445.2 2.7 multiply_reduce_fusion.2
  447.9 0.7 rev.7
  450.1 58.2 %all-reduce.26 = f32[64]{0:T(128)S(1)} all-reduce(f32[64]{0:T(128)S(1)} %dynamic-update-slice.6), channel_id=4, replica_groups=mesh['ctx'=32,'head'=8] {'ctx'}, use_global_device_ids=true, to_apply=%add.26 | all-reduce | flops 64 | bytes 512
  508.4 1.4 while.20
  509.9 0.7 rev.8
  512.1 40.4 %reduce-scatter.4.cloned.1.call-done = f32[128,128]{1,0:T(8,128)} async-done(((f32[1024,128]{1,0:T(8,128)}), f32[128,128]{1,0:T(8,128)}) %reduce-scatter.4.cloned.1.call-update) | async-done | bytes 65552 | tf_op jit(solution)/shard_map/reduce_scatter | solution.py:245
  (280 shorter events, 33.5 us)
Async XLA Ops:
  7.2 321.0 %reduce-scatter.6.cloned.1.call-start = ((), (), s32[]{:S(2)}) async-start(), calls=%async_computation.4 | async-start | bytes 4325376 | tf_op jit(solution)/shard_map/reduce_scatter | solution.py:229
  82.8 26.2 %copy-start = (bf16[1024,256]{0,1:T(8,128)(2,1)}, bf16[1024,256]{0,1:T(8,128)(2,1)S(1)}, u32[]{:S(2)}) copy-start(bf16[1024,256]{0,1:T(8,128)(2,1)S(1)} %copy.181) | copy-start | bytes 1572868
  84.1 9.3 %copy-start.6 = (f32[1024,128]{0,1:T(8,128)}, f32[1024,128]{0,1:T(8,128)S(1)}, u32[]{:S(2)}) copy-start(f32[1024,128]{0,1:T(8,128)S(1)} %copy.202) | copy-start | bytes 1572868
  84.2 33.6 %copy-start.40 = (s32[8]{0:T(128)}, s32[8]{0:T(128)S(1)}, u32[]{:S(2)}) copy-start(s32[8]{0:T(128)S(1)} %pad_add_fusion.2) | copy-start | bytes 100
  86.3 4.2 copy-start.23
  86.3 31.6 %copy-start.22 = (f32[2,8,128]{2,1,0:T(8,128)}, f32[2,8,128]{2,1,0:T(8,128)S(1)}, u32[]{:S(2)}) copy-start(f32[2,8,128]{2,1,0:T(8,128)S(1)} %get-tuple-element.220) | copy-start | bytes 24580
  87.7 2.9 copy-start.25
  91.3 2.1 copy-start.14
  92.2 3.9 copy-start.34
  96.0 7.9 %copy-start.35 = (pred[5,32]{1,0:T(8,128)(4,1)}, pred[5,32]{1,0:T(8,128)(4,1)S(1)}, u32[]{:S(2)}) copy-start(pred[5,32]{1,0:T(8,128)(4,1)S(1)} %stack.5) | copy-start | bytes 484
  99.5 4.7 copy-start.11
  99.6 4.8 copy-start.19
  103.9 5.4 copy-start.17
  103.9 14.0 %copy-start.16 = (bf16[1024,256]{1,0:T(8,128)(2,1)S(1)}, bf16[1024,256]{1,0:T(8,128)(2,1)}, u32[]{:S(2)}) copy-start(bf16[1024,256]{1,0:T(8,128)(2,1)} %param.11) | copy-start | bytes 1572868
  104.0 319.8 %all-gather.5.cloned.1.call-start = ((), (), s32[]{:S(2)}) async-start(), calls=%async_computation.6 | async-start | bytes 4325376 | tf_op jit(solution)/shard_map/all_gather | solution.py:210
  104.3 248.9 %copy-start.4 = (f32[1024,128]{1,0:T(8,128)}, f32[1024,128]{1,0:T(8,128)S(1)}, u32[]{:S(2)}) copy-start(f32[1024,128]{1,0:T(8,128)S(1)} %convert_element_type.14) | copy-start | bytes 1572868
  107.1 20.8 %copy-start.29 = (f32[8,2]{1,0:T(8,128)}, f32[8,2]{1,0:T(8,128)S(1)}, u32[]{:S(2)}) copy-start(f32[8,2]{1,0:T(8,128)S(1)} %gather_fusion.12) | copy-start | bytes 196
  118.2 219.0 %copy-start.2 = (bf16[2,1024,128]{2,1,0:T(8,128)(2,1)}, bf16[2,1024,128]{2,1,0:T(8,128)(2,1)S(1)}, u32[]{:S(2)}) copy-start(bf16[2,1024,128]{2,1,0:T(8,128)(2,1)S(1)} %copy.174) | copy-start | bytes 1572868
  121.0 0.6 copy-start.36
  123.3 4.6 copy-start.12
  123.5 0.6 copy-start.37
  124.2 205.0 %copy-start.27 = (f32[2,1,1,512]{3,0,2,1:T(2,128)}, f32[2,1,1,512]{3,0,2,1:T(2,128)S(1)}, u32[]{:S(2)}) copy-start(f32[2,1,1,512]{3,0,2,1:T(2,128)S(1)} %copy.281) | copy-start | bytes 12292
  127.9 201.3 %copy-start.38 = (f32[2]{0:T(128)}, f32[2]{0:T(128)S(1)}, u32[]{:S(2)}) copy-start(f32[2]{0:T(128)S(1)} %fusion.96) | copy-start | bytes 28
  330.2 7.7 %copy-start.39 = (f32[2]{0:T(128)S(1)}, f32[2]{0:T(128)}, u32[]{:S(2)}) copy-start(f32[2]{0:T(128)} %copy-done.38) | copy-start | bytes 28
  334.4 10.1 %copy-start.30 = (f32[8,2]{1,0:T(8,128)S(1)}, f32[8,2]{1,0:T(8,128)}, u32[]{:S(2)}) copy-start(f32[8,2]{1,0:T(8,128)} %copy-done.29) | copy-start | bytes 196
  334.4 10.1 %copy-start.41 = (pred[8]{0:T(512)(128)(4,1)S(1)}, pred[8]{0:T(512)(128)(4,1)}, u32[]{:S(2)}) copy-start(pred[8]{0:T(512)(128)(4,1)} %get-tuple-element.246) | copy-start | bytes 28
  337.2 5.9 %copy-start.9 = (f32[2,4,128,128]{3,2,1,0:T(8,128)}, f32[2,4,128,128]{3,2,1,0:T(8,128)S(1)}, u32[]{:S(2)}) copy-start(f32[2,4,128,128]{3,2,1,0:T(8,128)S(1)} %get-tuple-element.231) | copy-start | bytes 1572868
  337.9 5.2 copy-start.13
  338.7 173.4 %reduce-scatter.8.cloned.1.call-start = ((), (), s32[]{:S(2)}) async-start(), calls=%async_computation.5 | async-start | bytes 589824 | tf_op jit(solution)/shard_map/reduce_scatter | solution.py:246
  341.2 14.4 %copy-start.20 = (f32[2,8,128]{2,1,0:T(8,128)S(1)}, f32[2,8,128]{2,1,0:T(8,128)}, u32[]{:S(2)}) copy-start(f32[2,8,128]{2,1,0:T(8,128)} %get-tuple-element.208) | copy-start | bytes 24580
  353.3 9.7 %copy-start.10 = (f32[2,4,128,128]{3,2,1,0:T(8,128)S(1)}, f32[2,4,128,128]{3,2,1,0:T(8,128)}, u32[]{:S(2)}) copy-start(f32[2,4,128,128]{3,2,1,0:T(8,128)} %copy-done.9) | copy-start | bytes 1572868
  355.6 4.2 copy-start.5
  355.6 11.2 %copy-start.28 = (f32[2,1,1,512]{3,0,2,1:T(2,128)S(1)}, f32[2,1,1,512]{3,0,2,1:T(2,128)}, u32[]{:S(2)}) copy-start(f32[2,1,1,512]{3,0,2,1:T(2,128)} %copy-done.27) | copy-start | bytes 12292
  386.7 10.5 %copy-start.3 = (bf16[2,1024,128]{2,1,0:T(8,128)(2,1)S(1)}, bf16[2,1024,128]{2,1,0:T(8,128)(2,1)}, u32[]{:S(2)}) copy-start(bf16[2,1024,128]{2,1,0:T(8,128)(2,1)} %copy-done.2) | copy-start | bytes 1572868
  392.5 9.2 %copy-start.18 = (bf16[1024,128]{1,0:T(8,128)(2,1)S(1)}, bf16[1024,128]{1,0:T(8,128)(2,1)}, u32[]{:S(2)}) copy-start(bf16[1024,128]{1,0:T(8,128)(2,1)} %param.10) | copy-start | bytes 786436
  397.2 24.8 %copy-start.33 = (f32[2,512]{1,0:T(2,128)S(1)}, f32[2,512]{1,0:T(2,128)}, u32[]{:S(2)}) copy-start(f32[2,512]{1,0:T(2,128)} %get-tuple-element.201) | copy-start | bytes 12292
  397.2 24.8 %copy-start.32 = (f32[2,2,256]{2,1,0:T(2,128)S(1)}, f32[2,2,256]{2,1,0:T(2,128)}, u32[]{:S(2)}) copy-start(f32[2,2,256]{2,1,0:T(2,128)} %get-tuple-element.203) | copy-start | bytes 12292
  401.6 29.1 %copy-start.1 = (bf16[1024,256]{0,1:T(8,128)(2,1)S(1)}, bf16[1024,256]{0,1:T(8,128)(2,1)}, u32[]{:S(2)}) copy-start(bf16[1024,256]{0,1:T(8,128)(2,1)} %copy-done) | copy-start | bytes 1572868
  423.7 128.8 %reduce-scatter.4.cloned.1.call-start = ((), (), s32[]{:S(2)}) async-start(), calls=%async_computation.3 | async-start | bytes 589824 | tf_op jit(solution)/shard_map/reduce_scatter | solution.py:245
  430.6 2.4 copy-start.7
  430.6 2.4 copy-start.15
  433.0 4.5 copy-start.21
  437.5 7.7 %copy-start.8 = (f32[1024,128]{0,1:T(8,128)S(1)}, f32[1024,128]{0,1:T(8,128)}, u32[]{:S(2)}) copy-start(f32[1024,128]{0,1:T(8,128)} %copy-done.6) | copy-start | bytes 1572868
  443.6 64.8 %copy-start.31 = (f32[2]{0:T(128)S(1)}, f32[2]{0:T(128)}, u32[]{:S(2)}) copy-start(f32[2]{0:T(128)} %custom-call) | copy-start | bytes 28
  443.6 67.0 %copy-start.24 = (f32[2,8,128]{2,1,0:T(8,128)S(1)}, f32[2,8,128]{2,1,0:T(8,128)}, u32[]{:S(2)}) copy-start(f32[2,8,128]{2,1,0:T(8,128)} %copy-done.23) | copy-start | bytes 24580
  443.6 67.0 %copy-start.26 = (pred[1024]{0:T(1024)(128)(4,1)S(1)}, pred[1024]{0:T(1024)(128)(4,1)}, u32[]{:S(2)}) copy-start(pred[1024]{0:T(1024)(128)(4,1)} %copy-done.25) | copy-start | bytes 3076
Sparse Core Ops, SparseCore 0:
  104.1 224.0 reduce-scatter.5
  338.8 82.5 all-gather.4
  424.6 33.6 reduce-scatter.7
  508.5 43.9 reduce-scatter.3
where the time goes:
time: 569 us; the launch traced here: 559 us
  waiting for transfers between devices  236 us (41%)
  blocking collectives  123 us (22%)
  local copies, waits for them, and re-layouts  78.4 us (14%)
  matrix products  69.6 us (12%)
  other arithmetic  29.9 us (5%)
  between operations  20.8 us (4%)
    reduce_scatter x1, waiting for transfers between devices, shards(): lax.psum_scatter(jnp.einsum('mnh,mhij->nhij', window, remote_grad, precis...  196 us
    unnamed x2, blocking collectives  123 us
    reduce_scatter x1, waiting for transfers between devices, shards(): lax.psum_scatter(jnp.sum(query_part, axis=0), 'head', scatter_dimension=0...  40.4 us
    dot_general x1, matrix products, shards(): jnp.einsum('ti,hti->ht', key_full, key_total, precision=PRECISE)  19.2 us
    pad x4, local copies, waits for them, and re-layouts, merge_blocks(): return blocks[0::2] * linkage[:, None, None] + blocks[1::2]  15.7 us
    dot_general x3, matrix products, stretch_mix(): jnp.einsum('cti,csi->cts', query_stretches, key_stretches, precision=PREC...  11.5 us
  transfers between devices with their start and end apart: 4, of which 2 were waited for; matrix products, arithmetic and copies ran while one was open for 24% of the time, Pallas kernels for 0%

commit v1 on v0

v1 whole, which is shorter than its diff:
```python
import functools

import jax
import jax.numpy as jnp
from jax import lax
from jax.experimental import pallas as pl
from jax.experimental.pallas import tpu as pltpu
from jax.sharding import PartitionSpec as P

STRETCH = 128
LOCAL_LEVELS = 3
EXTRA = 2
F32 = jnp.float32
BF16 = jnp.bfloat16


def halves(x):
    high = x.astype(BF16)
    return high, (x - high.astype(F32)).astype(BF16)


def thirds(x):
    high = x.astype(BF16)
    rest = x - high.astype(F32)
    middle = rest.astype(BF16)
    return high, middle, (rest - middle.astype(F32)).astype(BF16)


def dot(a, b):
    return jnp.dot(a, b, preferred_element_type=F32)


def dot_nt(a, b):
    return lax.dot_general(a, b, (((1,), (1,)), ((), ())), preferred_element_type=F32)


def dot_left(x, exact):
    high, low = halves(x)
    return dot(high, exact) + dot(low, exact)


def dot_right(exact, x):
    high, low = halves(x)
    return dot(exact, high) + dot(exact, low)


def sum_of(terms):
    return functools.reduce(jnp.add, terms)


def ones_where(mask):
    return jnp.where(mask, 1.0, 0.0).astype(BF16)


def part(c):
    return slice(c * STRETCH, (c + 1) * STRETCH)


def pop(number, bits):
    return sum_of([(number >> b) & 1 for b in range(bits)])


def kernel(
    n_ctx,
    n_head,
    q_ref,
    k_ref,
    v_ref,
    c_ref,
    g_ref,
    w_ref,
    s_ref,
    dq_ref,
    dk_ref,
    dv_ref,
    dg_ref,
    dw_ref,
    qt_ref,
    kt_ref,
    qtb_ref,
    ktb_ref,
    ctb_ref,
    block_ref,
    out1,
    buf1,
    out2,
    buf2,
    dqt_ref,
    dk_acc,
    head_out,
    head_in,
    sems,
):
    heads, tokens = g_ref.shape
    num = tokens // STRETCH
    rows = heads * num
    bits = n_ctx.bit_length() - 1
    slabs = EXTRA + bits
    slab_rows = buf1.shape[1]
    per_head = n_ctx // heads
    me = lax.axis_index("ctx")
    mine = lax.axis_index("head")
    count = pop(me, bits)
    everything = sum(EXTRA + bin(n).count("1") for n in range(n_ctx))

    barrier = pltpu.get_barrier_semaphore()

    def greet_ctx(k, _):
        pl.semaphore_signal(barrier, inc=1, device_id={"ctx": lax.rem(me + k, n_ctx)})
        return 0

    def greet_head(k, _):
        pl.semaphore_signal(barrier, inc=1, device_id={"head": lax.rem(mine + k, n_head)})
        return 0

    lax.fori_loop(1, n_ctx, greet_ctx, 0)
    lax.fori_loop(1, n_head, greet_head, 0)

    gates = jnp.concatenate(
        [g_ref[h : h + 1, part(c)] for h in range(heads) for c in range(num)], axis=0
    )
    seg_one = s_ref[...]
    seg = jnp.concatenate([seg_one] * heads, axis=0)
    row_at = lax.broadcasted_iota(jnp.int32, (STRETCH, STRETCH), 0)
    lane_at = lax.broadcasted_iota(jnp.int32, (STRETCH, STRETCH), 1)
    upto = ones_where(row_at <= lane_at)
    within = sum_of([dot(x, upto) for x in thirds(gates)])
    total = jnp.broadcast_to(within[:, STRETCH - 1 :], within.shape)
    seg_end = jnp.broadcast_to(seg[:, STRETCH - 1 :], seg.shape)
    seg_first = jnp.broadcast_to(seg_one[:, :1], seg_one.shape)[:1]
    ra = lax.broadcasted_iota(jnp.int32, (rows, rows), 0)
    rb = lax.broadcasted_iota(jnp.int32, (rows, rows), 1)
    same_head = (ra // num) == (rb // num)
    earlier = ones_where(same_head & (rb < ra))
    later = ones_where(same_head & (rb > ra))
    before = sum_of([dot(earlier, x) for x in thirds(total)])
    entry = jnp.where(seg == seg_first, jnp.exp(within + before), 0.0)
    key_weight = jnp.where(seg == seg_end, jnp.exp(total - within), 0.0)
    through_exp = jnp.exp(total)

    def end(c):
        return seg_end[c : c + 1]

    def through(h, c):
        r = h * num + c
        return jnp.where(end(c - 1) == end(c), through_exp[r : r + 1], 0.0)

    def local_weight(h, level, c):
        r = h * num + c
        span = 1 << (level - 1)
        base = c // span * span
        shift = before[r : r + 1] - before[h * num + base : h * num + base + 1]
        return jnp.where(
            seg[r : r + 1] == end(base - 1), jnp.exp(within[r : r + 1] + shift), 0.0
        )

    def remote_row(h, k, c):
        picked = jnp.zeros((1, STRETCH), F32)
        for b in range(bits):
            is_it = (((me >> b) & 1) == 1) & (pop(me & ((1 << b) - 1), bits) == k)
            level = LOCAL_LEVELS + 1 + b
            picked = picked + jnp.where(is_it, w_ref[h, level : level + 1, part(c)], 0.0)
        return picked

    def columns(ref, h):
        return ref[:, h * STRETCH : (h + 1) * STRETCH]

    qt_ref[...] = q_ref[...].astype(F32).T
    kt_ref[...] = k_ref[...].astype(F32).T
    qtb_ref[...] = qt_ref[...].astype(BF16)
    ktb_ref[...] = kt_ref[...].astype(BF16)
    for h in range(heads):
        ctb_ref[h] = columns(c_ref, h).astype(F32).T.astype(BF16)

    for h in range(heads):
        for c in range(num):
            r = h * num + c
            scaled = kt_ref[:, part(c)] * key_weight[r : r + 1]
            block_ref[h, c] = dot_left(scaled, v_ref[part(c), h * STRETCH : (h + 1) * STRETCH])
        state = block_ref[h, 0]
        for c in range(1, num):
            state = through(h, c) * state + block_ref[h, c]
        last = h * num + num - 1
        passes = jnp.where(
            seg_first == end(num - 1), jnp.exp(before[last : last + 1] + total[last : last + 1]), 0.0
        )
        at = lax.broadcasted_iota(jnp.int32, (slab_rows, STRETCH), 0)
        meta = jnp.where(
            at == 0,
            passes,
            jnp.where(at == 1, seg_first.astype(F32), end(num - 1).astype(F32)),
        )
        for i in range(per_head):
            to = (h * per_head + i) * slabs
            out1[to] = meta
            out1[to + 1] = state[i * slab_rows : (i + 1) * slab_rows]

    for k in range(bits):

        @pl.when(count > k)
        def _(k=k):
            for h in range(heads):
                scaled = jnp.concatenate(
                    [
                        qt_ref[:, part(c)]
                        * (entry[h * num + c : h * num + c + 1] * remote_row(h, k, c))
                        for c in range(num)
                    ],
                    axis=1,
                )
                grad = dot_left(scaled, columns(c_ref, h))
                for i in range(per_head):
                    out1[(h * per_head + i) * slabs + EXTRA + k] = grad[
                        i * slab_rows : (i + 1) * slab_rows
                    ]

    pl.semaphore_wait(barrier, n_ctx + n_head - 2)

    for size in range(bits + 1):

        @pl.when(count == size)
        def _(size=size):
            def send(k, _):
                to = lax.rem(me + k, n_ctx)
                pltpu.make_async_remote_copy(
                    src_ref=out1.at[pl.ds(to * slabs, EXTRA + size)],
                    dst_ref=buf1.at[pl.ds(me * slabs, EXTRA + size)],
                    send_sem=sems.at[0],
                    recv_sem=sems.at[1],
                    device_id={"ctx": to},
                ).start()
                return 0

            lax.fori_loop(1, n_ctx, send, 0)
            for s in range(EXTRA + size):
                buf1[me * slabs + s] = out1[me * slabs + s]

    ones = jnp.ones((8, STRETCH), BF16)
    key_terms = [None] * rows
    query_terms = [None] * rows
    for c in range(num):
        seg_row = seg_one[c : c + 1]
        seg_col = jnp.broadcast_to(seg_row.astype(F32), (STRETCH, STRETCH)).T
        allowed = (row_at <= lane_at) & (seg_col == seg_row.astype(F32))
        scores = dot(k_ref[part(c), :], qtb_ref[:, part(c)])
        dk_sum = None
        dq_sum = None
        for h in range(heads):
            r = h * num + c
            cols = slice(h * STRETCH, (h + 1) * STRETCH)
            w_row = within[r : r + 1]
            w_col = jnp.broadcast_to(w_row, (STRETCH, STRETCH)).T
            decay = jnp.where(allowed, jnp.exp(jnp.minimum(w_row - w_col, 0.0)), 0.0)
            pairs = dot(v_ref[part(c), cols], ctb_ref[h, :, part(c)])
            mixed = decay * scores
            weight = w_ref[h, 0:1, part(c)]
            d_weight = jnp.sum(mixed * pairs, axis=0, keepdims=True)
            dw_ref[h, 0:1, part(c)] = d_weight
            query_terms[r] = weight * d_weight
            dv_ref[part(c), cols] = dot_left(mixed * weight, c_ref[part(c), cols])
            d_scores = decay * pairs * weight
            dk_one = dot_left(d_scores, q_ref[part(c), :])
            dq_one = dot_right(ktb_ref[:, part(c)], d_scores)
            products = k_ref[part(c), :].astype(F32) * dk_one
            key_terms[r] = sum_of([dot_nt(ones, x) for x in thirds(products)])[:1]
            dk_sum = dk_one if dk_sum is None else dk_sum + dk_one
            dq_sum = dq_one if dq_sum is None else dq_sum + dq_one
        dk_acc[part(c), :] = dk_sum
        dqt_ref[:, part(c)] = dq_sum

    for size in range(bits + 1):

        @pl.when(count == size)
        def _(size=size):
            got = buf1.at[pl.ds(0, everything - EXTRA - size)]
            pltpu.make_async_copy(got, got, sems.at[1]).wait()

    meta_rows = [[buf1[n * slabs, m : m + 1] for m in range(3)] for n in range(n_ctx)]
    enter = [None] + [
        jnp.where(meta_rows[n - 1][2] == meta_rows[n][1], 1.0, 0.0) for n in range(1, n_ctx)
    ]
    link = [jnp.zeros_like(meta_rows[0][0])] + [
        meta_rows[n][0] * enter[n] for n in range(1, n_ctx)
    ]

    def received(n, s):
        return buf1[n * slabs + s]

    def rank(n, b):
        return bin(n & ((1 << b) - 1)).count("1")

    blocks = [[received(n, 1) for n in range(n_ctx)]]
    passing = [link]
    for b in range(bits):
        low, thru = blocks[b], passing[b]
        half = len(low) // 2
        blocks.append([thru[2 * j + 1] * low[2 * j] + low[2 * j + 1] for j in range(half)])
        passing.append([thru[2 * j] * thru[2 * j + 1] for j in range(half)])
    block_grads = [[None] * (n_ctx >> b) for b in range(bits)]
    flows = [jnp.zeros((slab_rows, STRETCH), F32)] * n_ctx
    for b in range(bits):
        for j in range(1, n_ctx >> b, 2):
            lead = None
            for p in range(j << b, (j + 1) << b):
                lead = jnp.ones((1, STRETCH), F32) if lead is None else lead * link[p - 1]
                factor = lead * enter[p]
                remote = factor * blocks[b][j - 1]
                slot = EXTRA + rank(p, b)
                out2[p * slabs + slot] = remote
                grad = received(p, slot)
                flows[p] = flows[p] + remote * grad
                term = factor * grad
                old = block_grads[b][j - 1]
                block_grads[b][j - 1] = term if old is None else old + term
    down = [jnp.zeros((slab_rows, STRETCH), F32)]
    for b in reversed(range(bits)):
        next_down = []
        for j, top in enumerate(down):
            next_down += [block_grads[b][2 * j] + passing[b][2 * j + 1] * top, top]
        down = next_down
    after = jnp.zeros((slab_rows, STRETCH), F32)
    for n in reversed(range(n_ctx)):
        out2[n * slabs] = down[n]
        out2[n * slabs + 1] = after
        after = after + (flows[n] - received(n, 1) * down[n])

    def send_back(k, _):
        to = lax.rem(me + k, n_ctx)
        size_there = pop(to, bits)
        for size in range(bits + 1):

            @pl.when(size_there == size)
            def _(size=size):
                pltpu.make_async_remote_copy(
                    src_ref=out2.at[pl.ds(to * slabs, EXTRA + size)],
                    dst_ref=buf2.at[pl.ds(me * slabs, EXTRA + size)],
                    send_sem=sems.at[2],
                    recv_sem=sems.at[3],
                    device_id={"ctx": to},
                ).start()

        return 0

    lax.fori_loop(1, n_ctx, send_back, 0)
    for size in range(bits + 1):

        @pl.when(count == size)
        def _(size=size):
            for s in range(EXTRA + size):
                buf2[me * slabs + s] = out2[me * slabs + s]

    state_grads = []
    for h in range(heads):
        cols = slice(h * STRETCH, (h + 1) * STRETCH)
        lower = [block_ref[h, c] for c in range(num)]
        thru = [None] + [through(h, c) for c in range(1, num)]
        thru[0] = jnp.zeros_like(thru[1])
        per_level = []
        thrus = []
        for level in range(1, LOCAL_LEVELS + 1):
            span = 1 << (level - 1)
            grads = [None] * len(lower)
            for j in range(1, len(lower), 2):
                lanes = slice(j * span * STRETCH, (j + 1) * span * STRETCH)
                high, low = halves(lower[j - 1])
                reach = ctb_ref[h, :, lanes]
                got = dot(high, reach) + dot(low, reach)
                scaled = []
                for c in range(j * span, (j + 1) * span):
                    r = h * num + c
                    here = slice((c - j * span) * STRETCH, (c - j * span + 1) * STRETCH)
                    decay = local_weight(h, level, c)
                    q_part = qt_ref[:, part(c)]
                    d_weight = decay * jnp.sum(q_part * got[:, here], axis=0, keepdims=True)
                    weight = w_ref[h, level : level + 1, part(c)]
                    dw_ref[h, level : level + 1, part(c)] = d_weight
                    query_terms[r] = query_terms[r] + weight * d_weight
                    both = weight * decay
                    dqt_ref[:, part(c)] += both * got[:, here]
                    scaled.append(q_part * both)
                scaled = jnp.concatenate(scaled, axis=1) if span > 1 else scaled[0]
                grads[j - 1] = dot_left(scaled, c_ref[lanes, cols])
            for j in range(0, len(lower), 2):
                for c in range(j * span, (j + 1) * span):
                    dw_ref[h, level : level + 1, part(c)] = jnp.zeros((1, STRETCH), F32)
            per_level.append(grads)
            thrus.append(thru)
            lower, thru = (
                [thru[j + 1] * lower[j] + lower[j + 1] for j in range(0, len(lower), 2)],
                [thru[j] * thru[j + 1] for j in range(0, len(lower), 2)],
            )
        down = [None]
        for level in reversed(range(LOCAL_LEVELS)):
            next_down = []
            for j, top in enumerate(down):
                low = per_level[level][2 * j]
                next_down += [low if top is None else low + thrus[level][2 * j + 1] * top, top]
            down = next_down
        for c in range(num - 1):
            block_ref[h, c] = down[c]
        block_ref[h, num - 1] = jnp.zeros((STRETCH, STRETCH), F32)
        state_grads.append(None)

    for size in range(bits + 1):

        @pl.when(count == size)
        def _(size=size):
            got = buf2.at[pl.ds(0, (n_ctx - 1) * (EXTRA + size))]
            pltpu.make_async_copy(got, got, sems.at[3]).wait()

    def gathered(h, s):
        return jnp.concatenate(
            [buf2[(h * per_head + i) * slabs + s] for i in range(per_head)], axis=0
        )

    for h in range(heads):
        cols = slice(h * STRETCH, (h + 1) * STRETCH)
        top = gathered(h, 0)
        for c in reversed(range(num)):
            r = h * num + c
            seg_col = jnp.broadcast_to(seg_one[c : c + 1].astype(F32), (STRETCH, STRETCH)).T
            w_col = jnp.broadcast_to(within[r : r + 1], (STRETCH, STRETCH)).T
            weight = jnp.where(
                seg_col == end(c).astype(F32), jnp.exp(total[r : r + 1] - w_col), 0.0
            )
            high, low = halves(block_ref[h, c] + top)
            keys_here = k_ref[part(c), :]
            values_here = v_ref[part(c), cols]
            dv_ref[part(c), cols] += weight * (dot(keys_here, high) + dot(keys_here, low))
            dk_one = weight * (dot_nt(values_here, high) + dot_nt(values_here, low))
            dk_acc[part(c), :] += dk_one
            products = keys_here.astype(F32) * dk_one
            key_terms[r] = (
                key_terms[r] + sum_of([dot_nt(ones, x) for x in thirds(products)])[:1]
            )
            if c:
                top = through(h, c) * top

    for h in range(heads):
        dw_ref[h, LOCAL_LEVELS + 1 :, :] = jnp.zeros(
            (dw_ref.shape[1] - LOCAL_LEVELS - 1, tokens), F32
        )
    for k in range(bits):

        @pl.when(count > k)
        def _(k=k):
            for h in range(heads):
                high, low = halves(gathered(h, EXTRA + k))
                for c in range(num):
                    reach = ctb_ref[h, :, part(c)]
                    got = dot(high, reach) + dot(low, reach)
                    decay = entry[h * num + c : h * num + c + 1]
                    d_weight = decay * jnp.sum(qt_ref[:, part(c)] * got, axis=0, keepdims=True)
                    dqt_ref[:, part(c)] += (decay * remote_row(h, k, c)) * got
                    for b in range(bits):
                        is_it = (((me >> b) & 1) == 1) & (pop(me & ((1 << b) - 1), bits) == k)
                        level = LOCAL_LEVELS + 1 + b
                        dw_ref[h, level : level + 1, part(c)] += jnp.where(is_it, d_weight, 0.0)

    for c in range(num):
        head_out[c, :STRETCH] = dqt_ref[:, part(c)].T
        head_out[c, STRETCH:] = dk_acc[part(c), :]

    def send_head(k, _):
        to = lax.rem(mine + k, n_head)
        pltpu.make_async_remote_copy(
            src_ref=head_out.at[to],
            dst_ref=head_in.at[mine],
            send_sem=sems.at[4],
            recv_sem=sems.at[5],
            device_id={"head": to},
        ).start()
        return 0

    lax.fori_loop(1, n_head, send_head, 0)
    head_in[mine] = head_out[mine]

    from_here = ones_where(row_at >= lane_at)
    terms = []
    for h in range(heads):
        for c in range(num):
            r = h * num + c
            term = query_terms[r] - key_terms[r]
            for level in range(LOCAL_LEVELS + 1, LOCAL_LEVELS + 1 + bits):
                term = term + w_ref[h, level : level + 1, part(c)] * dw_ref[
                    h, level : level + 1, part(c)
                ]
            terms.append(term)
    terms = jnp.concatenate(terms, axis=0)
    suffix = sum_of([dot(x, from_here) for x in thirds(terms)])
    sums = jnp.broadcast_to(suffix[:, :1], suffix.shape)
    suffix = suffix + sum_of([dot(later, x) for x in thirds(sums)])
    for h in range(heads):
        beyond = sum_of([buf2[(h * per_head + i) * slabs + 1] for i in range(per_head)])
        beyond = jnp.sum(jnp.sum(beyond, axis=0, keepdims=True), axis=1, keepdims=True)
        for c in range(num):
            r = h * num + c
            dg_ref[h : h + 1, part(c)] = suffix[r : r + 1] + beyond

    for size in range(bits + 1):

        @pl.when(count == size)
        def _(size=size):
            sent = out1.at[pl.ds(0, (n_ctx - 1) * (EXTRA + size))]
            pltpu.make_async_copy(sent, sent, sems.at[0]).wait()
            sent = out2.at[pl.ds(0, everything - EXTRA - size)]
            pltpu.make_async_copy(sent, sent, sems.at[2]).wait()

    others = head_in.at[pl.ds(0, n_head - 1)]
    pltpu.make_async_copy(others, others, sems.at[5]).wait()
    pltpu.make_async_copy(others, others, sems.at[4]).wait()
    dq_ref[...] = sum_of([head_in[n, :STRETCH] for n in range(n_head)])
    dk_ref[...] = sum_of([head_in[n, STRETCH:] for n in range(n_head)])


def shards(queries, keys, values, gates, level_weights, segment, cotangent):
    n_ctx, n_head = lax.axis_size("ctx"), lax.axis_size("head")
    heads, tokens = gates.shape
    num = tokens // STRETCH
    bits = n_ctx.bit_length() - 1
    slab_rows = heads * STRETCH // n_ctx
    held = pltpu.VMEM((n_ctx * (EXTRA + bits), slab_rows, STRETCH), F32)
    turned = pltpu.VMEM((STRETCH, tokens), F32)
    turned_half = pltpu.VMEM((STRETCH, tokens), BF16)
    chunks = pltpu.VMEM((n_head, 2 * STRETCH, STRETCH), F32)
    vmem = pl.BlockSpec(memory_space=pltpu.VMEM)
    rows_out = tokens // n_head
    return pl.pallas_call(
        functools.partial(kernel, n_ctx, n_head),
        out_shape=(
            jax.ShapeDtypeStruct((rows_out, STRETCH), F32),
            jax.ShapeDtypeStruct((rows_out, STRETCH), F32),
            jax.ShapeDtypeStruct(values.shape, F32),
            jax.ShapeDtypeStruct(gates.shape, F32),
            jax.ShapeDtypeStruct(level_weights.shape, F32),
        ),
        in_specs=[vmem] * 7,
        out_specs=(vmem,) * 5,
        scratch_shapes=[
            turned,
            turned,
            turned_half,
            turned_half,
            pltpu.VMEM((heads, STRETCH, tokens), BF16),
            pltpu.VMEM((heads, num, STRETCH, STRETCH), F32),
            held,
            held,
            held,
            held,
            turned,
            pltpu.VMEM((tokens, STRETCH), F32),
            chunks,
            chunks,
            pltpu.SemaphoreType.DMA((6,)),
        ],
        compiler_params=pltpu.CompilerParams(
            collective_id=0, has_side_effects=True, vmem_limit_bytes=40 * 2**20
        ),
        name="loglinear_backward",
    )(
        queries,
        keys,
        values,
        cotangent,
        gates,
        level_weights,
        segment.reshape(num, STRETCH),
    )


def solution(mesh):
    return jax.shard_map(
        shards,
        mesh=mesh,
        in_specs=(
            P("ctx", None),
            P("ctx", None),
            P("ctx", "head"),
            P("head", "ctx"),
            P("head", None, "ctx"),
            P("ctx"),
            P("ctx", "head"),
        ),
        out_specs=(
            P(("ctx", "head"), None),
            P(("ctx", "head"), None),
            P("ctx", "head"),
            P("head", "ctx"),
            P("head", None, "ctx"),
        ),
        check_vma=False,
    )
```

time: 569 us -> 70.3 us (0.12)
  the two profiles are of different devices: /device:TPU:1 before, /device:TPU:25 now
where the time goes in v1:
time: 70.3 us; the launch traced here: 70 us
  Pallas kernels  60.9 us (87%)
  local copies, waits for them, and re-layouts  8.44 us (12%)
    pallas_call x1, Pallas kernels, shards(): pl.pallas_call(functools.partial(kernel, n_ctx, n_head), out_shape=(jax.S...  60.9 us
    unnamed x17, local copies, waits for them, and re-layouts  7.74 us

profile of v1, /device:TPU:25, one launch (start us, length us, event | category | flops | bytes accessed | tf_op | source)
XLA Modules:
  0.0 70.0 jit_solution(15282938939911985757)
XLA Ops:
  0.6 0.0 copy-start.4
  0.6 0.0 copy-start.5
  0.7 0.9 %copy.12.w_ref = f32[2,10,1024]{2,1,0:T(8,128)S(1)} copy(f32[2,10,1024]{2,0,1:T(2,128)} %param.11) | data formatting | bytes 163840 | tf_op args[4]
  1.6 0.0 copy-done.4
  1.6 0.0 copy-done.5
  1.6 0.0 copy-start
  1.6 1.0 %copy-done = bf16[1024,256]{1,0:T(8,128)(2,1)S(1)} copy-done((bf16[1024,256]{1,0:T(8,128)(2,1)S(1)}, bf16[1024,256]{1,0:T(8,128)(2,1)}, u32[]{:S(2)}) %copy-start) | copy-done | bytes 524312
  2.6 0.0 copy-start.1
  2.7 1.0 %copy-done.1 = bf16[1024,256]{1,0:T(8,128)(2,1)S(1)} copy-done((bf16[1024,256]{1,0:T(8,128)(2,1)S(1)}, bf16[1024,256]{1,0:T(8,128)(2,1)}, u32[]{:S(2)}) %copy-start.1) | copy-done | bytes 524312
  3.7 0.0 copy-start.2
  3.7 0.9 %copy-done.2 = bf16[1024,128]{1,0:T(8,128)(2,1)S(1)} copy-done((bf16[1024,128]{1,0:T(8,128)(2,1)S(1)}, bf16[1024,128]{1,0:T(8,128)(2,1)}, u32[]{:S(2)}) %copy-start.2) | copy-done | bytes 262168
  4.6 0.0 copy-start.3
  4.6 0.9 %copy-done.3 = bf16[1024,128]{1,0:T(8,128)(2,1)S(1)} copy-done((bf16[1024,128]{1,0:T(8,128)(2,1)S(1)}, bf16[1024,128]{1,0:T(8,128)(2,1)}, u32[]{:S(2)}) %copy-start.3) | copy-done | bytes 262168
  5.6 60.9 %loglinear_backward.1 = (f32[128,128]{1,0:T(8,128)S(1)}, f32[128,128]{1,0:T(8,128)S(1)}, f32[1024,256]{1,0:T(8,128)S(1)}, f32[2,1024]{1,0:T(2,128)S(1)}, f32[2,10,1024]{2,1,0:T(8,128)S(1)}) custom-call(bf16[1024,128]{1,0:T(8,128)(2,1)S(1)} %copy-done.2, bf16[1024,128]{1,0:T(8,128)(2,1)S(1)} %copy-done.3, bf16[1024,256]{1,0:T(8,128)(2,1)S(1)} %copy-done, ...), custom_call_target="tpu_custom_call" | custom-call | tf_op jit(solution)/shard_map/loglinear_backward/pallas_call | solution.py:528
  66.5 0.7 %copy.13 = f32[2,10,1024]{2,0,1:T(2,128)} copy(f32[2,10,1024]{2,1,0:T(8,128)S(1)} %get-tuple-element.9) | data formatting | bytes 163840 | tf_op jit(solution)/shard_map/loglinear_backward/pallas_call | solution.py:528
  67.2 0.6 copy.18
  67.8 0.6 copy.19
  68.4 1.0 %copy.20 = f32[1024,256]{1,0:T(8,128)} copy(f32[1024,256]{1,0:T(8,128)S(1)} %get-tuple-element.17) | data formatting | bytes 2097152
  69.4 0.6 copy.21
Async XLA Ops:
  0.6 1.0 %copy-start.4 = (f32[2,1024]{1,0:T(2,128)S(1)}, f32[2,1024]{1,0:T(2,128)}, u32[]{:S(2)}) copy-start(f32[2,1024]{1,0:T(2,128)} %g_ref.1) | copy-start | bytes 24580
  0.6 1.0 %copy-start.5 = (s32[1024]{0:T(1024)S(1)}, s32[1024]{0:T(1024)}, u32[]{:S(2)}) copy-start(s32[1024]{0:T(1024)} %param.12) | copy-start | bytes 12292
  1.6 1.0 %copy-start = (bf16[1024,256]{1,0:T(8,128)(2,1)S(1)}, bf16[1024,256]{1,0:T(8,128)(2,1)}, u32[]{:S(2)}) copy-start(bf16[1024,256]{1,0:T(8,128)(2,1)} %v_ref.1) | copy-start | bytes 1572868
  2.6 1.0 %copy-start.1 = (bf16[1024,256]{1,0:T(8,128)(2,1)S(1)}, bf16[1024,256]{1,0:T(8,128)(2,1)}, u32[]{:S(2)}) copy-start(bf16[1024,256]{1,0:T(8,128)(2,1)} %c_ref.1) | copy-start | bytes 1572868
  3.7 0.9 %copy-start.2 = (bf16[1024,128]{1,0:T(8,128)(2,1)S(1)}, bf16[1024,128]{1,0:T(8,128)(2,1)}, u32[]{:S(2)}) copy-start(bf16[1024,128]{1,0:T(8,128)(2,1)} %q_ref.1) | copy-start | bytes 786436
  4.6 0.9 %copy-start.3 = (bf16[1024,128]{1,0:T(8,128)(2,1)S(1)}, bf16[1024,128]{1,0:T(8,128)(2,1)}, u32[]{:S(2)}) copy-start(bf16[1024,128]{1,0:T(8,128)(2,1)} %k_ref.1) | copy-start | bytes 786436

commit v2 on v1

--- a/solution.py
+++ b/solution.py
@@ -9,7 +9,7 @@
 
 STRETCH = 128
 LOCAL_LEVELS = 3
-EXTRA = 2
+EXTRA = 1
 F32 = jnp.float32
 BF16 = jnp.bfloat16
 
@@ -63,6 +63,23 @@
 def kernel(
     n_ctx,
     n_head,
+    q_in,
+    k_in,
+    v_in,
+    c_in,
+    g_in,
+    w_in,
+    s_in,
+    dq_out,
+    dk_out,
+    dv_out,
+    dg_out,
+    dw_out,
+    dq_ref,
+    dk_ref,
+    dv_ref,
+    dg_ref,
+    dw_ref,
     q_ref,
     k_ref,
     v_ref,
@@ -70,11 +87,6 @@
     g_ref,
     w_ref,
     s_ref,
-    dq_ref,
-    dk_ref,
-    dv_ref,
-    dg_ref,
-    dw_ref,
     qt_ref,
     kt_ref,
     qtb_ref,
@@ -87,10 +99,34 @@
     buf2,
     dqt_ref,
     dk_acc,
+    meta_out,
+    meta_in,
+    flow_out,
+    flow_in,
     head_out,
+    pair_in,
     head_in,
     sems,
+    pair_sems,
+    in_sems,
+    out_sems,
 ):
+    loads = [
+        pltpu.make_async_copy(source, target, in_sems.at[i])
+        for i, (source, target) in enumerate(
+            [
+                (g_in, g_ref),
+                (s_in, s_ref),
+                (k_in, k_ref),
+                (v_in, v_ref),
+                (q_in, q_ref),
+                (c_in, c_ref),
+                (w_in, w_ref),
+            ]
+        )
+    ]
+    for load in loads:
+        load.start()
     heads, tokens = g_ref.shape
     num = tokens // STRETCH
     rows = heads * num
@@ -115,6 +151,9 @@
 
     lax.fori_loop(1, n_ctx, greet_ctx, 0)
     lax.fori_loop(1, n_head, greet_head, 0)
+
+    for load in loads[:2]:
+        load.wait()
 
     gates = jnp.concatenate(
         [g_ref[h : h + 1, part(c)] for h in range(heads) for c in range(num)], axis=0
@@ -159,11 +198,14 @@
         for b in range(bits):
             is_it = (((me >> b) & 1) == 1) & (pop(me & ((1 << b) - 1), bits) == k)
             level = LOCAL_LEVELS + 1 + b
-            picked = picked + jnp.where(is_it, w_ref[h, level : level + 1, part(c)], 0.0)
+            picked = picked + jnp.where(is_it, w_ref[level, h : h + 1, part(c)], 0.0)
         return picked
 
     def columns(ref, h):
         return ref[:, h * STRETCH : (h + 1) * STRETCH]
+
+    for load in loads[2:]:
+        load.wait()
 
     qt_ref[...] = q_ref[...].astype(F32).T
     kt_ref[...] = k_ref[...].astype(F32).T
@@ -184,16 +226,15 @@
         passes = jnp.where(
             seg_first == end(num - 1), jnp.exp(before[last : last + 1] + total[last : last + 1]), 0.0
         )
-        at = lax.broadcasted_iota(jnp.int32, (slab_rows, STRETCH), 0)
-        meta = jnp.where(
-            at == 0,
+        at = lax.broadcasted_iota(jnp.int32, (1, STRETCH), 1)
+        meta_out[h] = jnp.where(
+            at < 32,
             passes,
-            jnp.where(at == 1, seg_first.astype(F32), end(num - 1).astype(F32)),
+            jnp.where(at < 64, seg_first.astype(F32), end(num - 1).astype(F32)),
         )
         for i in range(per_head):
             to = (h * per_head + i) * slabs
-            out1[to] = meta
-            out1[to + 1] = state[i * slab_rows : (i + 1) * slab_rows]
+            out1[to] = state[i * slab_rows : (i + 1) * slab_rows]
 
     for k in range(bits):
 
@@ -215,6 +256,20 @@
                     ]
 
     pl.semaphore_wait(barrier, n_ctx + n_head - 2)
+
+    def send_meta(k, _):
+        to = lax.rem(me + k, n_ctx)
+        pltpu.make_async_remote_copy(
+            src_ref=meta_out.at[to // per_head],
+            dst_ref=meta_in.at[me],
+            send_sem=sems.at[6],
+            recv_sem=sems.at[7],
+            device_id={"ctx": to},
+        ).start()
+        return 0
+
+    lax.fori_loop(1, n_ctx, send_meta, 0)
+    meta_in[me] = meta_out[me // per_head]
 
     for size in range(bits + 1):
 
@@ -253,9 +308,9 @@
             decay = jnp.where(allowed, jnp.exp(jnp.minimum(w_row - w_col, 0.0)), 0.0)
             pairs = dot(v_ref[part(c), cols], ctb_ref[h, :, part(c)])
             mixed = decay * scores
-            weight = w_ref[h, 0:1, part(c)]
+            weight = w_ref[0, h : h + 1, part(c)]
             d_weight = jnp.sum(mixed * pairs, axis=0, keepdims=True)
-            dw_ref[h, 0:1, part(c)] = d_weight
+            dw_ref[0, h : h + 1, part(c)] = d_weight
             query_terms[r] = weight * d_weight
             dv_ref[part(c), cols] = dot_left(mixed * weight, c_ref[part(c), cols])
             d_scores = decay * pairs * weight
@@ -275,7 +330,12 @@
             got = buf1.at[pl.ds(0, everything - EXTRA - size)]
             pltpu.make_async_copy(got, got, sems.at[1]).wait()
 
-    meta_rows = [[buf1[n * slabs, m : m + 1] for m in range(3)] for n in range(n_ctx)]
+    got_meta = meta_in.at[pl.ds(0, n_ctx - 1)]
+    pltpu.make_async_copy(got_meta, got_meta, sems.at[7]).wait()
+    meta_rows = [
+        [jnp.broadcast_to(meta_in[n][:, i : i + 1], (1, STRETCH)) for i in (0, 32, 64)]
+        for n in range(n_ctx)
+    ]
     enter = [None] + [
         jnp.where(meta_rows[n - 1][2] == meta_rows[n][1], 1.0, 0.0) for n in range(1, n_ctx)
     ]
@@ -289,7 +349,7 @@
     def rank(n, b):
         return bin(n & ((1 << b) - 1)).count("1")
 
-    blocks = [[received(n, 1) for n in range(n_ctx)]]
+    blocks = [[received(n, 0) for n in range(n_ctx)]]
     passing = [link]
     for b in range(bits):
         low, thru = blocks[b], passing[b]
@@ -321,11 +381,18 @@
     after = jnp.zeros((slab_rows, STRETCH), F32)
     for n in reversed(range(n_ctx)):
         out2[n * slabs] = down[n]
-        out2[n * slabs + 1] = after
-        after = after + (flows[n] - received(n, 1) * down[n])
+        flow_out[n] = jnp.sum(after, axis=0, keepdims=True)
+        after = after + (flows[n] - received(n, 0) * down[n])
 
     def send_back(k, _):
         to = lax.rem(me + k, n_ctx)
+        pltpu.make_async_remote_copy(
+            src_ref=flow_out.at[to],
+            dst_ref=flow_in.at[me],
+            send_sem=sems.at[8],
+            recv_sem=sems.at[9],
+            device_id={"ctx": to},
+        ).start()
         size_there = pop(to, bits)
         for size in range(bits + 1):
 
@@ -342,6 +409,7 @@
         return 0
 
     lax.fori_loop(1, n_ctx, send_back, 0)
+    flow_in[me] = flow_out[me]
     for size in range(bits + 1):
 
         @pl.when(count == size)
@@ -372,8 +440,8 @@
                     decay = local_weight(h, level, c)
                     q_part = qt_ref[:, part(c)]
                     d_weight = decay * jnp.sum(q_part * got[:, here], axis=0, keepdims=True)
-                    weight = w_ref[h, level : level + 1, part(c)]
-                    dw_ref[h, level : level + 1, part(c)] = d_weight
+                    weight = w_ref[level, h : h + 1, part(c)]
+                    dw_ref[level, h : h + 1, part(c)] = d_weight
                     query_terms[r] = query_terms[r] + weight * d_weight
                     both = weight * decay
                     dqt_ref[:, part(c)] += both * got[:, here]
@@ -382,7 +450,7 @@
                 grads[j - 1] = dot_left(scaled, c_ref[lanes, cols])
             for j in range(0, len(lower), 2):
                 for c in range(j * span, (j + 1) * span):
-                    dw_ref[h, level : level + 1, part(c)] = jnp.zeros((1, STRETCH), F32)
+                    dw_ref[level, h : h + 1, part(c)] = jnp.zeros((1, STRETCH), F32)
             per_level.append(grads)
             thrus.append(thru)
             lower, thru = (
@@ -436,10 +504,9 @@
             if c:
                 top = through(h, c) * top
 
-    for h in range(heads):
-        dw_ref[h, LOCAL_LEVELS + 1 :, :] = jnp.zeros(
-            (dw_ref.shape[1] - LOCAL_LEVELS - 1, tokens), F32
-        )
+    dw_ref[LOCAL_LEVELS + 1 :] = jnp.zeros(
+        (dw_ref.shape[0] - LOCAL_LEVELS - 1, heads, tokens), F32
+    )
     for k in range(bits):
 
         @pl.when(count > k)
@@ -455,26 +522,50 @@
                     for b in range(bits):
                         is_it = (((me >> b) & 1) == 1) & (pop(me & ((1 << b) - 1), bits) == k)
                         level = LOCAL_LEVELS + 1 + b
-                        dw_ref[h, level : level + 1, part(c)] += jnp.where(is_it, d_weight, 0.0)
+                        dw_ref[level, h : h + 1, part(c)] += jnp.where(is_it, d_weight, 0.0)
+
+    def store(i, source, target):
+        copy = pltpu.make_async_copy(source, target, out_sems.at[i])
+        copy.start()
+        return copy
+
+    stores = [store(2, dv_ref, dv_out), store(4, dw_ref, dw_out)]
 
     for c in range(num):
         head_out[c, :STRETCH] = dqt_ref[:, part(c)].T
         head_out[c, STRETCH:] = dk_acc[part(c), :]
 
-    def send_head(k, _):
-        to = lax.rem(mine + k, n_head)
+    n_chip = n_head // 2
+    core, chip = lax.rem(mine, 2), mine // 2
+    sibling = chip * 2 + 1 - core
+    for x in range(n_chip):
         pltpu.make_async_remote_copy(
-            src_ref=head_out.at[to],
-            dst_ref=head_in.at[mine],
+            src_ref=head_out.at[2 * x + 1 - core],
+            dst_ref=pair_in.at[x],
+            send_sem=pair_sems.at[0, x],
+            recv_sem=pair_sems.at[1, x],
+            device_id={"head": sibling},
+        ).start()
+
+    def join(x):
+        pltpu.make_async_copy(pair_in.at[x], pair_in.at[x], pair_sems.at[1, x]).wait()
+        pair_in[x] = pair_in[x] + head_out[2 * x + core]
+
+    for k in range(1, n_chip):
+        x = lax.rem(chip + k, n_chip)
+        join(x)
+        pltpu.make_async_remote_copy(
+            src_ref=pair_in.at[x],
+            dst_ref=head_in.at[chip],
             send_sem=sems.at[4],
             recv_sem=sems.at[5],
-            device_id={"head": to},
+            device_id={"head": x * 2 + core},
         ).start()
-        return 0
-
-    lax.fori_loop(1, n_head, send_head, 0)
-    head_in[mine] = head_out[mine]
-
+    join(chip)
+    head_in[chip] = pair_in[chip]
+
+    got_flow = flow_in.at[pl.ds(0, n_ctx - 1)]
+    pltpu.make_async_copy(got_flow, got_flow, sems.at[9]).wait()
     from_here = ones_where(row_at >= lane_at)
     terms = []
     for h in range(heads):
@@ -482,8 +573,8 @@
             r = h * num + c
             term = query_terms[r] - key_terms[r]
             for level in range(LOCAL_LEVELS + 1, LOCAL_LEVELS + 1 + bits):
-                term = term + w_ref[h, level : level + 1, part(c)] * dw_ref[
-                    h, level : level + 1, part(c)
+                term = term + w_ref[level, h : h + 1, part(c)] * dw_ref[
+                    level, h : h + 1, part(c)
                 ]
             terms.append(term)
     terms = jnp.concatenate(terms, axis=0)
@@ -491,11 +582,12 @@
     sums = jnp.broadcast_to(suffix[:, :1], suffix.shape)
     suffix = suffix + sum_of([dot(later, x) for x in thirds(sums)])
     for h in range(heads):
-        beyond = sum_of([buf2[(h * per_head + i) * slabs + 1] for i in range(per_head)])
-        beyond = jnp.sum(jnp.sum(beyond, axis=0, keepdims=True), axis=1, keepdims=True)
+        beyond = sum_of([flow_in[h * per_head + i] for i in range(per_head)])
+        beyond = jnp.sum(beyond, axis=1, keepdims=True)
         for c in range(num):
             r = h * num + c
             dg_ref[h : h + 1, part(c)] = suffix[r : r + 1] + beyond
+    stores.append(store(3, dg_ref, dg_out))
 
     for size in range(bits + 1):
 
@@ -506,11 +598,46 @@
             sent = out2.at[pl.ds(0, everything - EXTRA - size)]
             pltpu.make_async_copy(sent, sent, sems.at[2]).wait()
 
-    others = head_in.at[pl.ds(0, n_head - 1)]
+    sent = meta_in.at[pl.ds(0, n_ctx - 1)]
+    pltpu.make_async_copy(sent, sent, sems.at[6]).wait()
+    pltpu.make_async_copy(sent, sent, sems.at[8]).wait()
+    for x in range(n_chip):
+        pltpu.make_async_copy(pair_in.at[x], pair_in.at[x], pair_sems.at[0, x]).wait()
+
+    others = head_in.at[pl.ds(0, n_chip - 1)]
     pltpu.make_async_copy(others, others, sems.at[5]).wait()
     pltpu.make_async_copy(others, others, sems.at[4]).wait()
-    dq_ref[...] = sum_of([head_in[n, :STRETCH] for n in range(n_head)])
-    dk_ref[...] = sum_of([head_in[n, STRETCH:] for n in range(n_head)])
+    dq_ref[...] = sum_of([head_in[n, :STRETCH] for n in range(n_chip)])
+    dk_ref[...] = sum_of([head_in[n, STRETCH:] for n in range(n_chip)])
+    stores.append(store(0, dq_ref, dq_out))
+    stores.append(store(1, dk_ref, dk_out))
+    for copy in stores:
+        copy.wait()
+
+
+def finish(pieces, *refs):
+    half = len(pieces)
+    given, results, held = refs[:half], refs[half : 2 * half], refs[2 * half : 3 * half]
+    load_sems, store_sems = refs[3 * half :]
+    steps = []
+    for ref, out, mid, count in zip(given, results, held, pieces):
+        size = ref.shape[0] // count
+        for at in range(count):
+            cut = pl.ds(at * size, size)
+            i = len(steps)
+            steps.append(
+                (
+                    pltpu.make_async_copy(ref.at[cut], mid.at[cut], load_sems.at[i]),
+                    pltpu.make_async_copy(mid.at[cut], out.at[cut], store_sems.at[i]),
+                )
+            )
+    for load, _ in steps:
+        load.start()
+    for load, store in steps:
+        load.wait()
+        store.start()
+    for _, store in steps:
+        store.wait()
 
 
 def shards(queries, keys, values, gates, level_weights, segment, cotangent):
@@ -522,21 +649,29 @@
     held = pltpu.VMEM((n_ctx * (EXTRA + bits), slab_rows, STRETCH), F32)
     turned = pltpu.VMEM((STRETCH, tokens), F32)
     turned_half = pltpu.VMEM((STRETCH, tokens), BF16)
-    chunks = pltpu.VMEM((n_head, 2 * STRETCH, STRETCH), F32)
-    vmem = pl.BlockSpec(memory_space=pltpu.VMEM)
+
+    def chunks(n):
+        return pltpu.VMEM((n, 2 * STRETCH, STRETCH), F32)
+
+    anywhere = pl.BlockSpec(memory_space=pl.ANY)
     rows_out = tokens // n_head
-    return pl.pallas_call(
+    weights = level_weights.transpose(1, 0, 2)
+    segments = segment.reshape(num, STRETCH)
+    inputs = (queries, keys, values, cotangent, gates, weights, segments)
+    results = (
+        jax.ShapeDtypeStruct((rows_out, STRETCH), F32),
+        jax.ShapeDtypeStruct((rows_out, STRETCH), F32),
+        jax.ShapeDtypeStruct(values.shape, F32),
+        jax.ShapeDtypeStruct(gates.shape, F32),
+        jax.ShapeDtypeStruct(weights.shape, F32),
+    )
+    raw = pl.pallas_call(
         functools.partial(kernel, n_ctx, n_head),
-        out_shape=(
-            jax.ShapeDtypeStruct((rows_out, STRETCH), F32),
-            jax.ShapeDtypeStruct((rows_out, STRETCH), F32),
-            jax.ShapeDtypeStruct(values.shape, F32),
-            jax.ShapeDtypeStruct(gates.shape, F32),
-            jax.ShapeDtypeStruct(level_weights.shape, F32),
-        ),
-        in_specs=[vmem] * 7,
-        out_specs=(vmem,) * 5,
+        out_shape=results,
+        in_specs=[anywhere] * 7,
+        out_specs=(anywhere,) * 5,
         scratch_shapes=[
+            *[pltpu.VMEM(x.shape, x.dtype) for x in (*results, *inputs)],
             turned,
             turned,
             turned_half,
@@ -549,23 +684,37 @@
             held,
             turned,
             pltpu.VMEM((tokens, STRETCH), F32),
-            chunks,
-            chunks,
-            pltpu.SemaphoreType.DMA((6,)),
+            pltpu.VMEM((heads, 1, STRETCH), F32),
+            pltpu.VMEM((n_ctx, 1, STRETCH), F32),
+            pltpu.VMEM((n_ctx, 1, STRETCH), F32),
+            pltpu.VMEM((n_ctx, 1, STRETCH), F32),
+            chunks(n_head),
+            chunks(n_head // 2),
+            chunks(n_head // 2),
+            pltpu.SemaphoreType.DMA((10,)),
+            pltpu.SemaphoreType.DMA((2, n_head // 2)),
+            pltpu.SemaphoreType.DMA((7,)),
+            pltpu.SemaphoreType.DMA((5,)),
         ],
         compiler_params=pltpu.CompilerParams(
-            collective_id=0, has_side_effects=True, vmem_limit_bytes=40 * 2**20
+            collective_id=0, has_side_effects=True, vmem_limit_bytes=56 * 2**20
         ),
         name="loglinear_backward",
-    )(
-        queries,
-        keys,
-        values,
-        cotangent,
-        gates,
-        level_weights,
-        segment.reshape(num, STRETCH),
-    )
+    )(*inputs)
+    pieces = (1, 1, 4, 1, 1)
+    *outs, weight_grad = pl.pallas_call(
+        functools.partial(finish, pieces),
+        out_shape=[jax.ShapeDtypeStruct(x.shape, F32) for x in raw],
+        in_specs=[anywhere] * len(raw),
+        out_specs=[anywhere] * len(raw),
+        scratch_shapes=[
+            *[pltpu.VMEM(x.shape, F32) for x in raw],
+            pltpu.SemaphoreType.DMA((sum(pieces),)),
+            pltpu.SemaphoreType.DMA((sum(pieces),)),
+        ],
+        name="store_results",
+    )(*raw)
+    return (*outs, weight_grad.transpose(1, 0, 2))
 
 
 def solution(mesh):

time: 70.3 us -> 57.3 us (0.82)
  local copies, waits for them, and re-layouts: 8.44 us -> 0 us
  Pallas kernels: 60.9 us -> 56.5 us
    unnamed x17 -> x0, local copies, waits for them, and re-layouts: 7.74 us -> none
    pallas_call x1 -> x2, Pallas kernels: 60.9 us -> 56.5 us  [the longest x1 54.4 us: shards(): pl.pallas_call(functools.partial(kernel, n_ctx, n_head), out_shape=result...]
where the time goes in v2:
time: 57.3 us; the launch traced here: 57.2 us
  Pallas kernels  56.5 us (99%)
  between operations  0.64 us (1%)
    pallas_call x1, Pallas kernels, shards(): pl.pallas_call(functools.partial(kernel, n_ctx, n_head), out_shape=result...  54.4 us
    pallas_call x1, Pallas kernels, shards(): pl.pallas_call(functools.partial(finish, pieces), out_shape=[jax.ShapeDty...  2.15 us

profile of v2, /device:TPU:25, one launch (start us, length us, event | category | flops | bytes accessed | tf_op | source)
XLA Modules:
  0.0 57.2 jit_solution(14069582438576527507)
XLA Ops:
  0.6 54.4 %loglinear_backward.1 = (f32[128,128]{1,0:T(8,128)}, f32[128,128]{1,0:T(8,128)}, f32[1024,256]{1,0:T(8,128)}, f32[2,1024]{1,0:T(2,128)}, f32[10,2,1024]{2,1,0:T(2,128)}) custom-call(bf16[1024,128]{1,0:T(8,128)(2,1)} %q_in.1, bf16[1024,128]{1,0:T(8,128)(2,1)} %k_in.1, bf16[1024,256]{1,0:T(8,128)(2,1)} %v_in.1, bf16[1024,256]{1,0:T(8,128)(2,1)} %c_in.1, ...), custom_call_target="tpu_custom_call" | custom-call | tf_op jit(solution)/shard_map/loglinear_backward/pallas_call | solution.py:668
  55.0 2.2 %store_results.1 = (f32[128,128]{1,0:T(8,128)}, f32[128,128]{1,0:T(8,128)}, f32[1024,256]{1,0:T(8,128)}, f32[2,1024]{1,0:T(2,128)}, f32[10,2,1024]{2,1,0:T(2,128)}) custom-call(f32[128,128]{1,0:T(8,128)} %get-tuple-element.15.refs_0_, f32[128,128]{1,0:T(8,128)} %get-tuple-element.16.refs_1_, f32[1024,256]{1,0:T(8,128)} %get-tuple-element.17.refs_2_, ...), custom_call_target="tpu_custom_call" | custom-call | tf_op jit(solution)/shard_map/store_results/pallas_call | solution.py:705

commit v3 on v2

--- a/solution.py
+++ b/solution.py
@@ -9,7 +9,6 @@
 
 STRETCH = 128
 LOCAL_LEVELS = 3
-EXTRA = 1
 F32 = jnp.float32
 BF16 = jnp.bfloat16
 
@@ -93,10 +92,14 @@
     ktb_ref,
     ctb_ref,
     block_ref,
+    s_out,
+    s_in_buf,
     out1,
     buf1,
     out2,
     buf2,
+    t_out,
+    t_in,
     dqt_ref,
     dk_acc,
     meta_out,
@@ -131,13 +134,17 @@
     num = tokens // STRETCH
     rows = heads * num
     bits = n_ctx.bit_length() - 1
-    slabs = EXTRA + bits
+    slabs = bits
     slab_rows = buf1.shape[1]
     per_head = n_ctx // heads
     me = lax.axis_index("ctx")
     mine = lax.axis_index("head")
     count = pop(me, bits)
-    everything = sum(EXTRA + bin(n).count("1") for n in range(n_ctx))
+    everything = sum(bin(n).count("1") for n in range(n_ctx))
+
+    def partner(k):
+        step = (k + 1) // 2
+        return lax.rem(jnp.where(lax.rem(k, 2) == 1, me + step, me + n_ctx - step), n_ctx)
 
     barrier = pltpu.get_barrier_semaphore()
 
@@ -233,8 +240,31 @@
             jnp.where(at < 64, seg_first.astype(F32), end(num - 1).astype(F32)),
         )
         for i in range(per_head):
-            to = (h * per_head + i) * slabs
-            out1[to] = state[i * slab_rows : (i + 1) * slab_rows]
+            s_out[h * per_head + i] = state[i * slab_rows : (i + 1) * slab_rows]
+
+    pl.semaphore_wait(barrier, n_ctx + n_head - 2)
+
+    def send_state(k, _):
+        to = partner(k)
+        pltpu.make_async_remote_copy(
+            src_ref=meta_out.at[to // per_head],
+            dst_ref=meta_in.at[me],
+            send_sem=sems.at[6],
+            recv_sem=sems.at[7],
+            device_id={"ctx": to},
+        ).start()
+        pltpu.make_async_remote_copy(
+            src_ref=s_out.at[to],
+            dst_ref=s_in_buf.at[me],
+            send_sem=sems.at[10],
+            recv_sem=sems.at[11],
+            device_id={"ctx": to},
+        ).start()
+        return 0
+
+    lax.fori_loop(1, n_ctx, send_state, 0)
+    meta_in[me] = meta_out[me // per_head]
+    s_in_buf[me] = s_out[me]
 
     for k in range(bits):
 
@@ -251,35 +281,19 @@
                 )
                 grad = dot_left(scaled, columns(c_ref, h))
                 for i in range(per_head):
-                    out1[(h * per_head + i) * slabs + EXTRA + k] = grad[
+                    out1[(h * per_head + i) * slabs + k] = grad[
                         i * slab_rows : (i + 1) * slab_rows
                     ]
 
-    pl.semaphore_wait(barrier, n_ctx + n_head - 2)
-
-    def send_meta(k, _):
-        to = lax.rem(me + k, n_ctx)
-        pltpu.make_async_remote_copy(
-            src_ref=meta_out.at[to // per_head],
-            dst_ref=meta_in.at[me],
-            send_sem=sems.at[6],
-            recv_sem=sems.at[7],
-            device_id={"ctx": to},
-        ).start()
-        return 0
-
-    lax.fori_loop(1, n_ctx, send_meta, 0)
-    meta_in[me] = meta_out[me // per_head]
-
-    for size in range(bits + 1):
+    for size in range(1, bits + 1):
 
         @pl.when(count == size)
         def _(size=size):
             def send(k, _):
-                to = lax.rem(me + k, n_ctx)
+                to = partner(k)
                 pltpu.make_async_remote_copy(
-                    src_ref=out1.at[pl.ds(to * slabs, EXTRA + size)],
-                    dst_ref=buf1.at[pl.ds(me * slabs, EXTRA + size)],
+                    src_ref=out1.at[pl.ds(to * slabs, size)],
+                    dst_ref=buf1.at[pl.ds(me * slabs, size)],
                     send_sem=sems.at[0],
                     recv_sem=sems.at[1],
                     device_id={"ctx": to},
@@ -287,8 +301,66 @@
                 return 0
 
             lax.fori_loop(1, n_ctx, send, 0)
-            for s in range(EXTRA + size):
+            for s in range(size):
                 buf1[me * slabs + s] = out1[me * slabs + s]
+
+    got_state = s_in_buf.at[pl.ds(0, n_ctx - 1)]
+    pltpu.make_async_copy(got_state, got_state, sems.at[11]).wait()
+    got_meta = meta_in.at[pl.ds(0, n_ctx - 1)]
+    pltpu.make_async_copy(got_meta, got_meta, sems.at[7]).wait()
+    meta_rows = [
+        [jnp.broadcast_to(meta_in[n][:, i : i + 1], (1, STRETCH)) for i in (0, 32, 64)]
+        for n in range(n_ctx)
+    ]
+    enter = [None] + [
+        jnp.where(meta_rows[n - 1][2] == meta_rows[n][1], 1.0, 0.0) for n in range(1, n_ctx)
+    ]
+    link = [jnp.zeros_like(meta_rows[0][0])] + [
+        meta_rows[n][0] * enter[n] for n in range(1, n_ctx)
+    ]
+
+    def rank(n, b):
+        return bin(n & ((1 << b) - 1)).count("1")
+
+    blocks = [s_in_buf[n] for n in range(n_ctx)]
+    passing = [link]
+    factors = {}
+    for b in range(bits):
+        thru = passing[b]
+        for j in range(1, n_ctx >> b, 2):
+            lead = None
+            for p in range(j << b, (j + 1) << b):
+                lead = jnp.ones((1, STRETCH), F32) if lead is None else lead * link[p - 1]
+                factors[b, p] = lead * enter[p]
+                out2[p * slabs + rank(p, b)] = factors[b, p] * blocks[j - 1]
+        half = len(blocks) // 2
+        blocks = [thru[2 * j + 1] * blocks[2 * j] + blocks[2 * j + 1] for j in range(half)]
+        passing.append([thru[2 * j] * thru[2 * j + 1] for j in range(half)])
+
+    def send_buckets(k, _):
+        to = partner(k)
+        size_there = pop(to, bits)
+        for size in range(1, bits + 1):
+
+            @pl.when(size_there == size)
+            def _(size=size):
+                pltpu.make_async_remote_copy(
+                    src_ref=out2.at[pl.ds(to * slabs, size)],
+                    dst_ref=buf2.at[pl.ds(me * slabs, size)],
+                    send_sem=sems.at[2],
+                    recv_sem=sems.at[3],
+                    device_id={"ctx": to},
+                ).start()
+
+        return 0
+
+    lax.fori_loop(1, n_ctx, send_buckets, 0)
+    for size in range(1, bits + 1):
+
+        @pl.when(count == size)
+        def _(size=size):
+            for s in range(size):
+                buf2[me * slabs + s] = out2[me * slabs + s]
 
     ones = jnp.ones((8, STRETCH), BF16)
     key_terms = [None] * rows
@@ -327,49 +399,18 @@
 
         @pl.when(count == size)
         def _(size=size):
-            got = buf1.at[pl.ds(0, everything - EXTRA - size)]
+            got = buf1.at[pl.ds(0, everything - size)]
             pltpu.make_async_copy(got, got, sems.at[1]).wait()
 
-    got_meta = meta_in.at[pl.ds(0, n_ctx - 1)]
-    pltpu.make_async_copy(got_meta, got_meta, sems.at[7]).wait()
-    meta_rows = [
-        [jnp.broadcast_to(meta_in[n][:, i : i + 1], (1, STRETCH)) for i in (0, 32, 64)]
-        for n in range(n_ctx)
-    ]
-    enter = [None] + [
-        jnp.where(meta_rows[n - 1][2] == meta_rows[n][1], 1.0, 0.0) for n in range(1, n_ctx)
-    ]
-    link = [jnp.zeros_like(meta_rows[0][0])] + [
-        meta_rows[n][0] * enter[n] for n in range(1, n_ctx)
-    ]
-
-    def received(n, s):
-        return buf1[n * slabs + s]
-
-    def rank(n, b):
-        return bin(n & ((1 << b) - 1)).count("1")
-
-    blocks = [[received(n, 0) for n in range(n_ctx)]]
-    passing = [link]
-    for b in range(bits):
-        low, thru = blocks[b], passing[b]
-        half = len(low) // 2
-        blocks.append([thru[2 * j + 1] * low[2 * j] + low[2 * j + 1] for j in range(half)])
-        passing.append([thru[2 * j] * thru[2 * j + 1] for j in range(half)])
     block_grads = [[None] * (n_ctx >> b) for b in range(bits)]
     flows = [jnp.zeros((slab_rows, STRETCH), F32)] * n_ctx
     for b in range(bits):
         for j in range(1, n_ctx >> b, 2):
-            lead = None
             for p in range(j << b, (j + 1) << b):
-                lead = jnp.ones((1, STRETCH), F32) if lead is None else lead * link[p - 1]
-                factor = lead * enter[p]
-                remote = factor * blocks[b][j - 1]
-                slot = EXTRA + rank(p, b)
-                out2[p * slabs + slot] = remote
-                grad = received(p, slot)
-                flows[p] = flows[p] + remote * grad
-                term = factor * grad
+                slot = p * slabs + rank(p, b)
+                grad = buf1[slot]
+                flows[p] = flows[p] + out2[slot] * grad
+                term = factors[b, p] * grad
                 old = block_grads[b][j - 1]
                 block_grads[b][j - 1] = term if old is None else old + term
     down = [jnp.zeros((slab_rows, STRETCH), F32)]
@@ -380,12 +421,19 @@
         down = next_down
     after = jnp.zeros((slab_rows, STRETCH), F32)
     for n in reversed(range(n_ctx)):
-        out2[n * slabs] = down[n]
+        t_out[n] = down[n]
         flow_out[n] = jnp.sum(after, axis=0, keepdims=True)
-        after = after + (flows[n] - received(n, 0) * down[n])
-
-    def send_back(k, _):
-        to = lax.rem(me + k, n_ctx)
+        after = after + (flows[n] - s_in_buf[n] * down[n])
+
+    def send_grads(k, _):
+        to = partner(k)
+        pltpu.make_async_remote_copy(
+            src_ref=t_out.at[to],
+            dst_ref=t_in.at[me],
+            send_sem=sems.at[12],
+            recv_sem=sems.at[13],
+            device_id={"ctx": to},
+        ).start()
         pltpu.make_async_remote_copy(
             src_ref=flow_out.at[to],
             dst_ref=flow_in.at[me],
@@ -393,29 +441,11 @@
             recv_sem=sems.at[9],
             device_id={"ctx": to},
         ).start()
-        size_there = pop(to, bits)
-        for size in range(bits + 1):
-
-            @pl.when(size_there == size)
-            def _(size=size):
-                pltpu.make_async_remote_copy(
-                    src_ref=out2.at[pl.ds(to * slabs, EXTRA + size)],
-                    dst_ref=buf2.at[pl.ds(me * slabs, EXTRA + size)],
-                    send_sem=sems.at[2],
-                    recv_sem=sems.at[3],
-                    device_id={"ctx": to},
-                ).start()
-
         return 0
 
-    lax.fori_loop(1, n_ctx, send_back, 0)
+    lax.fori_loop(1, n_ctx, send_grads, 0)
+    t_in[me] = t_out[me]
     flow_in[me] = flow_out[me]
-    for size in range(bits + 1):
-
-        @pl.when(count == size)
-        def _(size=size):
-            for s in range(EXTRA + size):
-                buf2[me * slabs + s] = out2[me * slabs + s]
 
     state_grads = []
     for h in range(heads):
@@ -469,21 +499,44 @@
         block_ref[h, num - 1] = jnp.zeros((STRETCH, STRETCH), F32)
         state_grads.append(None)
 
-    for size in range(bits + 1):
+    for size in range(1, bits + 1):
 
         @pl.when(count == size)
         def _(size=size):
-            got = buf2.at[pl.ds(0, (n_ctx - 1) * (EXTRA + size))]
+            got = buf2.at[pl.ds(0, (n_ctx - 1) * size)]
             pltpu.make_async_copy(got, got, sems.at[3]).wait()
 
-    def gathered(h, s):
+    def gathered(ref, stride, s, h):
         return jnp.concatenate(
-            [buf2[(h * per_head + i) * slabs + s] for i in range(per_head)], axis=0
+            [ref[(h * per_head + i) * stride + s] for i in range(per_head)], axis=0
         )
+
+    dw_ref[LOCAL_LEVELS + 1 :] = jnp.zeros(
+        (dw_ref.shape[0] - LOCAL_LEVELS - 1, heads, tokens), F32
+    )
+    for k in range(bits):
+
+        @pl.when(count > k)
+        def _(k=k):
+            for h in range(heads):
+                high, low = halves(gathered(buf2, slabs, k, h))
+                for c in range(num):
+                    reach = ctb_ref[h, :, part(c)]
+                    got = dot(high, reach) + dot(low, reach)
+                    decay = entry[h * num + c : h * num + c + 1]
+                    d_weight = decay * jnp.sum(qt_ref[:, part(c)] * got, axis=0, keepdims=True)
+                    dqt_ref[:, part(c)] += (decay * remote_row(h, k, c)) * got
+                    for b in range(bits):
+                        is_it = (((me >> b) & 1) == 1) & (pop(me & ((1 << b) - 1), bits) == k)
+                        level = LOCAL_LEVELS + 1 + b
+                        dw_ref[level, h : h + 1, part(c)] += jnp.where(is_it, d_weight, 0.0)
+
+    got_grads = t_in.at[pl.ds(0, n_ctx - 1)]
+    pltpu.make_async_copy(got_grads, got_grads, sems.at[13]).wait()
 
     for h in range(heads):
         cols = slice(h * STRETCH, (h + 1) * STRETCH)
-        top = gathered(h, 0)
+        top = gathered(t_in, 1, 0, h)
         for c in reversed(range(num)):
             r = h * num + c
             seg_col = jnp.broadcast_to(seg_one[c : c + 1].astype(F32), (STRETCH, STRETCH)).T
@@ -503,26 +556,6 @@
             )
             if c:
                 top = through(h, c) * top
-
-    dw_ref[LOCAL_LEVELS + 1 :] = jnp.zeros(
-        (dw_ref.shape[0] - LOCAL_LEVELS - 1, heads, tokens), F32
-    )
-    for k in range(bits):
-
-        @pl.when(count > k)
-        def _(k=k):
-            for h in range(heads):
-                high, low = halves(gathered(h, EXTRA + k))
-                for c in range(num):
-                    reach = ctb_ref[h, :, part(c)]
-                    got = dot(high, reach) + dot(low, reach)
-                    decay = entry[h * num + c : h * num + c + 1]
-                    d_weight = decay * jnp.sum(qt_ref[:, part(c)] * got, axis=0, keepdims=True)
-                    dqt_ref[:, part(c)] += (decay * remote_row(h, k, c)) * got
-                    for b in range(bits):
-                        is_it = (((me >> b) & 1) == 1) & (pop(me & ((1 << b) - 1), bits) == k)
-                        level = LOCAL_LEVELS + 1 + b
-                        dw_ref[level, h : h + 1, part(c)] += jnp.where(is_it, d_weight, 0.0)
 
     def store(i, source, target):
         copy = pltpu.make_async_copy(source, target, out_sems.at[i])
@@ -593,14 +626,18 @@
 
         @pl.when(count == size)
         def _(size=size):
-            sent = out1.at[pl.ds(0, (n_ctx - 1) * (EXTRA + size))]
-            pltpu.make_async_copy(sent, sent, sems.at[0]).wait()
-            sent = out2.at[pl.ds(0, everything - EXTRA - size)]
+            if size:
+                sent = out1.at[pl.ds(0, (n_ctx - 1) * size)]
+                pltpu.make_async_copy(sent, sent, sems.at[0]).wait()
+            sent = out2.at[pl.ds(0, everything - size)]
             pltpu.make_async_copy(sent, sent, sems.at[2]).wait()
 
     sent = meta_in.at[pl.ds(0, n_ctx - 1)]
     pltpu.make_async_copy(sent, sent, sems.at[6]).wait()
     pltpu.make_async_copy(sent, sent, sems.at[8]).wait()
+    sent = s_out.at[pl.ds(0, n_ctx - 1)]
+    pltpu.make_async_copy(sent, sent, sems.at[10]).wait()
+    pltpu.make_async_copy(sent, sent, sems.at[12]).wait()
     for x in range(n_chip):
         pltpu.make_async_copy(pair_in.at[x], pair_in.at[x], pair_sems.at[0, x]).wait()
 
@@ -646,7 +683,8 @@
     num = tokens // STRETCH
     bits = n_ctx.bit_length() - 1
     slab_rows = heads * STRETCH // n_ctx
-    held = pltpu.VMEM((n_ctx * (EXTRA + bits), slab_rows, STRETCH), F32)
+    held = pltpu.VMEM((n_ctx * bits, slab_rows, STRETCH), F32)
+    single = pltpu.VMEM((n_ctx, slab_rows, STRETCH), F32)
     turned = pltpu.VMEM((STRETCH, tokens), F32)
     turned_half = pltpu.VMEM((STRETCH, tokens), BF16)
 
@@ -678,10 +716,14 @@
             turned_half,
             pltpu.VMEM((heads, STRETCH, tokens), BF16),
             pltpu.VMEM((heads, num, STRETCH, STRETCH), F32),
+            single,
+            single,
             held,
             held,
             held,
             held,
+            single,
+            single,
             turned,
             pltpu.VMEM((tokens, STRETCH), F32),
             pltpu.VMEM((heads, 1, STRETCH), F32),
@@ -691,7 +733,7 @@
             chunks(n_head),
             chunks(n_head // 2),
             chunks(n_head // 2),
-            pltpu.SemaphoreType.DMA((10,)),
+            pltpu.SemaphoreType.DMA((14,)),
             pltpu.SemaphoreType.DMA((2, n_head // 2)),
             pltpu.SemaphoreType.DMA((7,)),
             pltpu.SemaphoreType.DMA((5,)),

time: 57.3 us -> 53.6 us (0.935)
  the two profiles are of different devices: /device:TPU:25 before, /device:TPU:1 now
where the time goes in v3:
time: 53.6 us; the launch traced here: 53.4 us
  Pallas kernels  52.6 us (98%)
  between operations  0.8 us (1%)
    pallas_call x1, Pallas kernels, shards(): pl.pallas_call(functools.partial(kernel, n_ctx, n_head), out_shape=result...  50.5 us
    pallas_call x1, Pallas kernels, shards(): pl.pallas_call(functools.partial(finish, pieces), out_shape=[jax.ShapeDty...  2.15 us

profile of v3, /device:TPU:1, one launch (start us, length us, event | category | flops | bytes accessed | tf_op | source)
XLA Modules:
  0.0 53.4 jit_solution(12105480910678032576)
XLA Ops:
  0.6 50.5 %loglinear_backward.1 = (f32[128,128]{1,0:T(8,128)}, f32[128,128]{1,0:T(8,128)}, f32[1024,256]{1,0:T(8,128)}, f32[2,1024]{1,0:T(2,128)}, f32[10,2,1024]{2,1,0:T(2,128)}) custom-call(bf16[1024,128]{1,0:T(8,128)(2,1)} %q_in.1, bf16[1024,128]{1,0:T(8,128)(2,1)} %k_in.1, bf16[1024,256]{1,0:T(8,128)(2,1)} %v_in.1, bf16[1024,256]{1,0:T(8,128)(2,1)} %c_in.1, ...), custom_call_target="tpu_custom_call" | custom-call | tf_op jit(solution)/shard_map/loglinear_backward/pallas_call | solution.py:706
  51.1 2.2 %store_results.1 = (f32[128,128]{1,0:T(8,128)}, f32[128,128]{1,0:T(8,128)}, f32[1024,256]{1,0:T(8,128)}, f32[2,1024]{1,0:T(2,128)}, f32[10,2,1024]{2,1,0:T(2,128)}) custom-call(f32[128,128]{1,0:T(8,128)} %get-tuple-element.15.refs_0_, f32[128,128]{1,0:T(8,128)} %get-tuple-element.16.refs_1_, f32[1024,256]{1,0:T(8,128)} %get-tuple-element.17.refs_2_, ...), custom_call_target="tpu_custom_call" | custom-call | tf_op jit(solution)/shard_map/store_results/pallas_call | solution.py:747

commit v4 on v3

--- a/solution.py
+++ b/solution.py
@@ -102,6 +102,7 @@
     t_in,
     dqt_ref,
     dk_acc,
+    product_ref,
     meta_out,
     meta_in,
     flow_out,
@@ -111,6 +112,7 @@
     head_in,
     sems,
     pair_sems,
+    chip_sems,
     in_sems,
     out_sems,
 ):
@@ -363,7 +365,6 @@
                 buf2[me * slabs + s] = out2[me * slabs + s]
 
     ones = jnp.ones((8, STRETCH), BF16)
-    key_terms = [None] * rows
     query_terms = [None] * rows
     for c in range(num):
         seg_row = seg_one[c : c + 1]
@@ -388,8 +389,7 @@
             d_scores = decay * pairs * weight
             dk_one = dot_left(d_scores, q_ref[part(c), :])
             dq_one = dot_right(ktb_ref[:, part(c)], d_scores)
-            products = k_ref[part(c), :].astype(F32) * dk_one
-            key_terms[r] = sum_of([dot_nt(ones, x) for x in thirds(products)])[:1]
+            product_ref[h, part(c), :] = k_ref[part(c), :].astype(F32) * dk_one
             dk_sum = dk_one if dk_sum is None else dk_sum + dk_one
             dq_sum = dq_one if dq_sum is None else dq_sum + dq_one
         dk_acc[part(c), :] = dk_sum
@@ -531,31 +531,79 @@
                         level = LOCAL_LEVELS + 1 + b
                         dw_ref[level, h : h + 1, part(c)] += jnp.where(is_it, d_weight, 0.0)
 
+    n_chip = n_head // 2
+    core, chip = lax.rem(mine, 2), mine // 2
+    sibling = chip * 2 + 1 - core
+
+    def send_pair(kind, x, source):
+        pltpu.make_async_remote_copy(
+            src_ref=source,
+            dst_ref=pair_in.at[kind, x],
+            send_sem=pair_sems.at[0, kind, x],
+            recv_sem=pair_sems.at[1, kind, x],
+            device_id={"head": sibling},
+        ).start()
+
+    def join(kind, x):
+        arrived = pair_in.at[kind, x]
+        pltpu.make_async_copy(arrived, arrived, pair_sems.at[1, kind, x]).wait()
+        pair_in[kind, x] = pair_in[kind, x] + head_out[kind, 2 * x + core]
+
+    def send_chips(kind):
+        for k in range(1, n_chip):
+            x = lax.rem(chip + k, n_chip)
+            join(kind, x)
+            pltpu.make_async_remote_copy(
+                src_ref=pair_in.at[kind, x],
+                dst_ref=head_in.at[kind, chip],
+                send_sem=chip_sems.at[0, kind],
+                recv_sem=chip_sems.at[1, kind],
+                device_id={"head": x * 2 + core},
+            ).start()
+        join(kind, chip)
+        head_in[kind, chip] = pair_in[kind, chip]
+
+    def send_if_siblings(kind, c):
+        @pl.when(core != c % 2)
+        def _():
+            send_pair(kind, c // 2, head_out.at[kind, c])
+
+    for c in range(num):
+        head_out[0, c] = dqt_ref[:, part(c)].T
+        send_if_siblings(0, c)
+    send_chips(0)
+
     got_grads = t_in.at[pl.ds(0, n_ctx - 1)]
     pltpu.make_async_copy(got_grads, got_grads, sems.at[13]).wait()
 
+    tops = [gathered(t_in, 1, 0, h) for h in range(heads)]
+    reaches = []
     for h in range(heads):
-        cols = slice(h * STRETCH, (h + 1) * STRETCH)
-        top = gathered(t_in, 1, 0, h)
-        for c in reversed(range(num)):
+        to_end = [None] * num
+        to_end[num - 1] = jnp.ones((1, STRETCH), F32)
+        for c in reversed(range(num - 1)):
+            to_end[c] = to_end[c + 1] * through(h, c + 1)
+        reaches.append(to_end)
+    for c in range(num):
+        seg_col = jnp.broadcast_to(seg_one[c : c + 1].astype(F32), (STRETCH, STRETCH)).T
+        keys_here = k_ref[part(c), :]
+        dk_sum = dk_acc[part(c), :]
+        for h in range(heads):
+            cols = slice(h * STRETCH, (h + 1) * STRETCH)
             r = h * num + c
-            seg_col = jnp.broadcast_to(seg_one[c : c + 1].astype(F32), (STRETCH, STRETCH)).T
             w_col = jnp.broadcast_to(within[r : r + 1], (STRETCH, STRETCH)).T
             weight = jnp.where(
                 seg_col == end(c).astype(F32), jnp.exp(total[r : r + 1] - w_col), 0.0
             )
-            high, low = halves(block_ref[h, c] + top)
-            keys_here = k_ref[part(c), :]
+            high, low = halves(block_ref[h, c] + reaches[h][c] * tops[h])
             values_here = v_ref[part(c), cols]
             dv_ref[part(c), cols] += weight * (dot(keys_here, high) + dot(keys_here, low))
             dk_one = weight * (dot_nt(values_here, high) + dot_nt(values_here, low))
-            dk_acc[part(c), :] += dk_one
-            products = keys_here.astype(F32) * dk_one
-            key_terms[r] = (
-                key_terms[r] + sum_of([dot_nt(ones, x) for x in thirds(products)])[:1]
-            )
-            if c:
-                top = through(h, c) * top
+            dk_sum = dk_sum + dk_one
+            product_ref[h, part(c), :] += keys_here.astype(F32) * dk_one
+        head_out[1, c] = dk_sum
+        send_if_siblings(1, c)
+    send_chips(1)
 
     def store(i, source, target):
         copy = pltpu.make_async_copy(source, target, out_sems.at[i])
@@ -563,39 +611,6 @@
         return copy
 
     stores = [store(2, dv_ref, dv_out), store(4, dw_ref, dw_out)]
-
-    for c in range(num):
-        head_out[c, :STRETCH] = dqt_ref[:, part(c)].T
-        head_out[c, STRETCH:] = dk_acc[part(c), :]
-
-    n_chip = n_head // 2
-    core, chip = lax.rem(mine, 2), mine // 2
-    sibling = chip * 2 + 1 - core
-    for x in range(n_chip):
-        pltpu.make_async_remote_copy(
-            src_ref=head_out.at[2 * x + 1 - core],
-            dst_ref=pair_in.at[x],
-            send_sem=pair_sems.at[0, x],
-            recv_sem=pair_sems.at[1, x],
-            device_id={"head": sibling},
-        ).start()
-
-    def join(x):
-        pltpu.make_async_copy(pair_in.at[x], pair_in.at[x], pair_sems.at[1, x]).wait()
-        pair_in[x] = pair_in[x] + head_out[2 * x + core]
-
-    for k in range(1, n_chip):
-        x = lax.rem(chip + k, n_chip)
-        join(x)
-        pltpu.make_async_remote_copy(
-            src_ref=pair_in.at[x],
-            dst_ref=head_in.at[chip],
-            send_sem=sems.at[4],
-            recv_sem=sems.at[5],
-            device_id={"head": x * 2 + core},
-        ).start()
-    join(chip)
-    head_in[chip] = pair_in[chip]
 
     got_flow = flow_in.at[pl.ds(0, n_ctx - 1)]
     pltpu.make_async_copy(got_flow, got_flow, sems.at[9]).wait()
@@ -604,7 +619,8 @@
     for h in range(heads):
         for c in range(num):
             r = h * num + c
-            term = query_terms[r] - key_terms[r]
+            sums = sum_of([dot_nt(ones, x) for x in thirds(product_ref[h, part(c), :])])
+            term = query_terms[r] - sums[:1]
             for level in range(LOCAL_LEVELS + 1, LOCAL_LEVELS + 1 + bits):
                 term = term + w_ref[level, h : h + 1, part(c)] * dw_ref[
                     level, h : h + 1, part(c)
@@ -638,14 +654,14 @@
     sent = s_out.at[pl.ds(0, n_ctx - 1)]
     pltpu.make_async_copy(sent, sent, sems.at[10]).wait()
     pltpu.make_async_copy(sent, sent, sems.at[12]).wait()
-    for x in range(n_chip):
-        pltpu.make_async_copy(pair_in.at[x], pair_in.at[x], pair_sems.at[0, x]).wait()
-
-    others = head_in.at[pl.ds(0, n_chip - 1)]
-    pltpu.make_async_copy(others, others, sems.at[5]).wait()
-    pltpu.make_async_copy(others, others, sems.at[4]).wait()
-    dq_ref[...] = sum_of([head_in[n, :STRETCH] for n in range(n_chip)])
-    dk_ref[...] = sum_of([head_in[n, STRETCH:] for n in range(n_chip)])
+    others = head_in.at[0, pl.ds(0, n_chip - 1)]
+    for kind, result in enumerate((dq_ref, dk_ref)):
+        for x in range(n_chip):
+            sent = pair_in.at[kind, x]
+            pltpu.make_async_copy(sent, sent, pair_sems.at[0, kind, x]).wait()
+        pltpu.make_async_copy(others, others, chip_sems.at[1, kind]).wait()
+        pltpu.make_async_copy(others, others, chip_sems.at[0, kind]).wait()
+        result[...] = sum_of([head_in[kind, n] for n in range(n_chip)])
     stores.append(store(0, dq_ref, dq_out))
     stores.append(store(1, dk_ref, dk_out))
     for copy in stores:
@@ -689,7 +705,7 @@
     turned_half = pltpu.VMEM((STRETCH, tokens), BF16)
 
     def chunks(n):
-        return pltpu.VMEM((n, 2 * STRETCH, STRETCH), F32)
+        return pltpu.VMEM((2, n, STRETCH, STRETCH), F32)
 
     anywhere = pl.BlockSpec(memory_space=pl.ANY)
     rows_out = tokens // n_head
@@ -726,6 +742,7 @@
             single,
             turned,
             pltpu.VMEM((tokens, STRETCH), F32),
+            pltpu.VMEM((heads, tokens, STRETCH), F32),
             pltpu.VMEM((heads, 1, STRETCH), F32),
             pltpu.VMEM((n_ctx, 1, STRETCH), F32),
             pltpu.VMEM((n_ctx, 1, STRETCH), F32),
@@ -734,7 +751,8 @@
             chunks(n_head // 2),
             chunks(n_head // 2),
             pltpu.SemaphoreType.DMA((14,)),
-            pltpu.SemaphoreType.DMA((2, n_head // 2)),
+            pltpu.SemaphoreType.DMA((2, 2, n_head // 2)),
+            pltpu.SemaphoreType.DMA((2, 2)),
             pltpu.SemaphoreType.DMA((7,)),
             pltpu.SemaphoreType.DMA((5,)),
         ],

time: 53.6 us -> 49 us (0.914)
  Pallas kernels: 52.6 us -> 48.3 us
    pallas_call x1, Pallas kernels: 50.5 us -> 46.1 us  [shards(): pl.pallas_call(functools.partial(kernel, n_ctx, n_head), out_shape=result...]
where the time goes in v4:
time: 49 us; the launch traced here: 48.9 us
  Pallas kernels  48.3 us (99%)
  between operations  0.64 us (1%)
    pallas_call x1, Pallas kernels, shards(): pl.pallas_call(functools.partial(kernel, n_ctx, n_head), out_shape=result...  46.1 us
    pallas_call x1, Pallas kernels, shards(): pl.pallas_call(functools.partial(finish, pieces), out_shape=[jax.ShapeDty...  2.15 us

profile of v4, /device:TPU:1, one launch (start us, length us, event | category | flops | bytes accessed | tf_op | source)
XLA Modules:
  0.0 48.9 jit_solution(900377698679120466)
XLA Ops:
  0.6 46.1 %loglinear_backward.1 = (f32[128,128]{1,0:T(8,128)}, f32[128,128]{1,0:T(8,128)}, f32[1024,256]{1,0:T(8,128)}, f32[2,1024]{1,0:T(2,128)}, f32[10,2,1024]{2,1,0:T(2,128)}) custom-call(bf16[1024,128]{1,0:T(8,128)(2,1)} %q_in.1, bf16[1024,128]{1,0:T(8,128)(2,1)} %k_in.1, bf16[1024,256]{1,0:T(8,128)(2,1)} %v_in.1, bf16[1024,256]{1,0:T(8,128)(2,1)} %c_in.1, ...), custom_call_target="tpu_custom_call" | custom-call | tf_op jit(solution)/shard_map/loglinear_backward/pallas_call | solution.py:722
  46.7 2.2 %store_results.1 = (f32[128,128]{1,0:T(8,128)}, f32[128,128]{1,0:T(8,128)}, f32[1024,256]{1,0:T(8,128)}, f32[2,1024]{1,0:T(2,128)}, f32[10,2,1024]{2,1,0:T(2,128)}) custom-call(f32[128,128]{1,0:T(8,128)} %get-tuple-element.15.refs_0_, f32[128,128]{1,0:T(8,128)} %get-tuple-element.16.refs_1_, f32[1024,256]{1,0:T(8,128)} %get-tuple-element.17.refs_2_, ...), custom_call_target="tpu_custom_call" | custom-call | tf_op jit(solution)/shard_map/store_results/pallas_call | solution.py:765

commit v5 on v4

--- a/solution.py
+++ b/solution.py
@@ -103,6 +103,7 @@
     dqt_ref,
     dk_acc,
     product_ref,
+    row_ref,
     meta_out,
     meta_in,
     flow_out,
@@ -213,15 +214,9 @@
     def columns(ref, h):
         return ref[:, h * STRETCH : (h + 1) * STRETCH]
 
-    for load in loads[2:]:
+    for load in loads[2:4]:
         load.wait()
-
-    qt_ref[...] = q_ref[...].astype(F32).T
     kt_ref[...] = k_ref[...].astype(F32).T
-    qtb_ref[...] = qt_ref[...].astype(BF16)
-    ktb_ref[...] = kt_ref[...].astype(BF16)
-    for h in range(heads):
-        ctb_ref[h] = columns(c_ref, h).astype(F32).T.astype(BF16)
 
     for h in range(heads):
         for c in range(num):
@@ -268,6 +263,10 @@
     meta_in[me] = meta_out[me // per_head]
     s_in_buf[me] = s_out[me]
 
+    for load in loads[4:]:
+        load.wait()
+    qt_ref[...] = q_ref[...].astype(F32).T
+
     for k in range(bits):
 
         @pl.when(count > k)
@@ -305,6 +304,11 @@
             lax.fori_loop(1, n_ctx, send, 0)
             for s in range(size):
                 buf1[me * slabs + s] = out1[me * slabs + s]
+
+    qtb_ref[...] = qt_ref[...].astype(BF16)
+    ktb_ref[...] = kt_ref[...].astype(BF16)
+    for h in range(heads):
+        ctb_ref[h] = columns(c_ref, h).astype(F32).T.astype(BF16)
 
     got_state = s_in_buf.at[pl.ds(0, n_ctx - 1)]
     pltpu.make_async_copy(got_state, got_state, sems.at[11]).wait()
@@ -403,27 +407,22 @@
             pltpu.make_async_copy(got, got, sems.at[1]).wait()
 
     block_grads = [[None] * (n_ctx >> b) for b in range(bits)]
-    flows = [jnp.zeros((slab_rows, STRETCH), F32)] * n_ctx
     for b in range(bits):
         for j in range(1, n_ctx >> b, 2):
-            for p in range(j << b, (j + 1) << b):
-                slot = p * slabs + rank(p, b)
-                grad = buf1[slot]
-                flows[p] = flows[p] + out2[slot] * grad
-                term = factors[b, p] * grad
-                old = block_grads[b][j - 1]
-                block_grads[b][j - 1] = term if old is None else old + term
+            block_grads[b][j - 1] = sum_of(
+                [
+                    factors[b, p] * buf1[p * slabs + rank(p, b)]
+                    for p in range(j << b, (j + 1) << b)
+                ]
+            )
     down = [jnp.zeros((slab_rows, STRETCH), F32)]
     for b in reversed(range(bits)):
         next_down = []
         for j, top in enumerate(down):
             next_down += [block_grads[b][2 * j] + passing[b][2 * j + 1] * top, top]
         down = next_down
-    after = jnp.zeros((slab_rows, STRETCH), F32)
-    for n in reversed(range(n_ctx)):
+    for n in range(n_ctx):
         t_out[n] = down[n]
-        flow_out[n] = jnp.sum(after, axis=0, keepdims=True)
-        after = after + (flows[n] - s_in_buf[n] * down[n])
 
     def send_grads(k, _):
         to = partner(k)
@@ -434,6 +433,20 @@
             recv_sem=sems.at[13],
             device_id={"ctx": to},
         ).start()
+        return 0
+
+    lax.fori_loop(1, n_ctx, send_grads, 0)
+    t_in[me] = t_out[me]
+
+    after = jnp.zeros((slab_rows, STRETCH), F32)
+    for n in reversed(range(n_ctx)):
+        flow_out[n] = jnp.sum(after, axis=0, keepdims=True)
+        after = after - s_in_buf[n] * t_out[n]
+        for slot in range(n * slabs, n * slabs + bin(n).count("1")):
+            after = after + out2[slot] * buf1[slot]
+
+    def send_flows(k, _):
+        to = partner(k)
         pltpu.make_async_remote_copy(
             src_ref=flow_out.at[to],
             dst_ref=flow_in.at[me],
@@ -443,8 +456,7 @@
         ).start()
         return 0
 
-    lax.fori_loop(1, n_ctx, send_grads, 0)
-    t_in[me] = t_out[me]
+    lax.fori_loop(1, n_ctx, send_flows, 0)
     flow_in[me] = flow_out[me]
 
     state_grads = []
@@ -549,19 +561,15 @@
         pltpu.make_async_copy(arrived, arrived, pair_sems.at[1, kind, x]).wait()
         pair_in[kind, x] = pair_in[kind, x] + head_out[kind, 2 * x + core]
 
-    def send_chips(kind):
-        for k in range(1, n_chip):
-            x = lax.rem(chip + k, n_chip)
-            join(kind, x)
-            pltpu.make_async_remote_copy(
-                src_ref=pair_in.at[kind, x],
-                dst_ref=head_in.at[kind, chip],
-                send_sem=chip_sems.at[0, kind],
-                recv_sem=chip_sems.at[1, kind],
-                device_id={"head": x * 2 + core},
-            ).start()
-        join(kind, chip)
-        head_in[kind, chip] = pair_in[kind, chip]
+    def send_chip(kind, x):
+        join(kind, x)
+        pltpu.make_async_remote_copy(
+            src_ref=pair_in.at[kind, x],
+            dst_ref=head_in.at[kind, chip],
+            send_sem=chip_sems.at[0, kind],
+            recv_sem=chip_sems.at[1, kind],
+            device_id={"head": x * 2 + core},
+        ).start()
 
     def send_if_siblings(kind, c):
         @pl.when(core != c % 2)
@@ -571,39 +579,56 @@
     for c in range(num):
         head_out[0, c] = dqt_ref[:, part(c)].T
         send_if_siblings(0, c)
-    send_chips(0)
+    for k in range(1, n_chip):
+        send_chip(0, lax.rem(chip + k, n_chip))
+    join(0, chip)
+    head_in[0, chip] = pair_in[0, chip]
+
+    for h in range(heads):
+        reach = jnp.ones((1, STRETCH), F32)
+        for c in reversed(range(num)):
+            r = h * num + c
+            row_ref[0, r] = within[r : r + 1]
+            row_ref[1, r] = total[r : r + 1]
+            row_ref[2, r] = end(c).astype(F32)
+            row_ref[3, r] = seg_one[c : c + 1].astype(F32)
+            row_ref[4, r] = reach
+            if c:
+                reach = reach * through(h, c)
 
     got_grads = t_in.at[pl.ds(0, n_ctx - 1)]
     pltpu.make_async_copy(got_grads, got_grads, sems.at[13]).wait()
-
     tops = [gathered(t_in, 1, 0, h) for h in range(heads)]
-    reaches = []
-    for h in range(heads):
-        to_end = [None] * num
-        to_end[num - 1] = jnp.ones((1, STRETCH), F32)
-        for c in reversed(range(num - 1)):
-            to_end[c] = to_end[c + 1] * through(h, c + 1)
-        reaches.append(to_end)
-    for c in range(num):
-        seg_col = jnp.broadcast_to(seg_one[c : c + 1].astype(F32), (STRETCH, STRETCH)).T
-        keys_here = k_ref[part(c), :]
-        dk_sum = dk_acc[part(c), :]
+
+    def finish_keys(c):
+        here = pl.ds(pl.multiple_of(c * STRETCH, STRETCH), STRETCH)
+        seg_col = jnp.broadcast_to(row_ref[3, c], (STRETCH, STRETCH)).T
+        keys_here = k_ref[here, :]
+        dk_sum = dk_acc[here, :]
         for h in range(heads):
             cols = slice(h * STRETCH, (h + 1) * STRETCH)
             r = h * num + c
-            w_col = jnp.broadcast_to(within[r : r + 1], (STRETCH, STRETCH)).T
+            w_col = jnp.broadcast_to(row_ref[0, r], (STRETCH, STRETCH)).T
             weight = jnp.where(
-                seg_col == end(c).astype(F32), jnp.exp(total[r : r + 1] - w_col), 0.0
+                seg_col == row_ref[2, r], jnp.exp(row_ref[1, r] - w_col), 0.0
             )
-            high, low = halves(block_ref[h, c] + reaches[h][c] * tops[h])
-            values_here = v_ref[part(c), cols]
-            dv_ref[part(c), cols] += weight * (dot(keys_here, high) + dot(keys_here, low))
+            high, low = halves(block_ref[h, c] + row_ref[4, r] * tops[h])
+            values_here = v_ref[here, cols]
+            dv_ref[here, cols] += weight * (dot(keys_here, high) + dot(keys_here, low))
             dk_one = weight * (dot_nt(values_here, high) + dot_nt(values_here, low))
             dk_sum = dk_sum + dk_one
-            product_ref[h, part(c), :] += keys_here.astype(F32) * dk_one
+            product_ref[h, here, :] += keys_here.astype(F32) * dk_one
         head_out[1, c] = dk_sum
-        send_if_siblings(1, c)
-    send_chips(1)
+
+    chip_order = [lax.rem(chip + k, n_chip) for k in range(1, n_chip + 1)]
+    for k, x in enumerate(chip_order):
+        finish_keys(2 * x + 1 - core)
+        send_pair(1, x, head_out.at[1, 2 * x + 1 - core])
+        finish_keys(2 * x + core)
+        if k:
+            send_chip(1, chip_order[k - 1])
+    join(1, chip)
+    head_in[1, chip] = pair_in[1, chip]
 
     def store(i, source, target):
         copy = pltpu.make_async_copy(source, target, out_sems.at[i])
@@ -743,6 +768,7 @@
             turned,
             pltpu.VMEM((tokens, STRETCH), F32),
             pltpu.VMEM((heads, tokens, STRETCH), F32),
+            pltpu.VMEM((5, heads * num, 1, STRETCH), F32),
             pltpu.VMEM((heads, 1, STRETCH), F32),
             pltpu.VMEM((n_ctx, 1, STRETCH), F32),
             pltpu.VMEM((n_ctx, 1, STRETCH), F32),

time: 49 us -> 48.3 us (0.986)
  Pallas kernels: 48.3 us -> 47.1 us
    pallas_call x1, Pallas kernels: 46.1 us -> 44.9 us  [shards(): pl.pallas_call(functools.partial(kernel, n_ctx, n_head), out_shape=result...]
where the time goes in v5:
time: 48.3 us; the launch traced here: 47.7 us
  Pallas kernels  47.1 us (98%)
  between operations  0.64 us (1%)
    pallas_call x1, Pallas kernels, shards(): pl.pallas_call(functools.partial(kernel, n_ctx, n_head), out_shape=result...  44.9 us
    pallas_call x1, Pallas kernels, shards(): pl.pallas_call(functools.partial(finish, pieces), out_shape=[jax.ShapeDty...  2.15 us

profile of v5, /device:TPU:1, one launch (start us, length us, event | category | flops | bytes accessed | tf_op | source)
XLA Modules:
  0.0 47.7 jit_solution(18116348000519386888)
XLA Ops:
  0.6 44.9 %loglinear_backward.1 = (f32[128,128]{1,0:T(8,128)}, f32[128,128]{1,0:T(8,128)}, f32[1024,256]{1,0:T(8,128)}, f32[2,1024]{1,0:T(2,128)}, f32[10,2,1024]{2,1,0:T(2,128)}) custom-call(bf16[1024,128]{1,0:T(8,128)(2,1)} %q_in.1, bf16[1024,128]{1,0:T(8,128)(2,1)} %k_in.1, bf16[1024,256]{1,0:T(8,128)(2,1)} %v_in.1, bf16[1024,256]{1,0:T(8,128)(2,1)} %c_in.1, ...), custom_call_target="tpu_custom_call" | custom-call | tf_op jit(solution)/shard_map/loglinear_backward/pallas_call | solution.py:747
  45.6 2.2 %store_results.1 = (f32[128,128]{1,0:T(8,128)}, f32[128,128]{1,0:T(8,128)}, f32[1024,256]{1,0:T(8,128)}, f32[2,1024]{1,0:T(2,128)}, f32[10,2,1024]{2,1,0:T(2,128)}) custom-call(f32[128,128]{1,0:T(8,128)} %get-tuple-element.15.refs_0_, f32[128,128]{1,0:T(8,128)} %get-tuple-element.16.refs_1_, f32[1024,256]{1,0:T(8,128)} %get-tuple-element.17.refs_2_, ...), custom_call_target="tpu_custom_call" | custom-call | tf_op jit(solution)/shard_map/store_results/pallas_call | solution.py:791

commit v6 on v5

--- a/solution.py
+++ b/solution.py
@@ -218,6 +218,28 @@
         load.wait()
     kt_ref[...] = k_ref[...].astype(F32).T
 
+    def send_state(h, k, _):
+        to = partner(k)
+
+        @pl.when(to // per_head == h)
+        def _():
+            pltpu.make_async_remote_copy(
+                src_ref=meta_out.at[h],
+                dst_ref=meta_in.at[me],
+                send_sem=sems.at[6],
+                recv_sem=sems.at[7],
+                device_id={"ctx": to},
+            ).start()
+            pltpu.make_async_remote_copy(
+                src_ref=s_out.at[to],
+                dst_ref=s_in_buf.at[me],
+                send_sem=sems.at[10],
+                recv_sem=sems.at[11],
+                device_id={"ctx": to},
+            ).start()
+
+        return 0
+
     for h in range(heads):
         for c in range(num):
             r = h * num + c
@@ -238,28 +260,10 @@
         )
         for i in range(per_head):
             s_out[h * per_head + i] = state[i * slab_rows : (i + 1) * slab_rows]
-
-    pl.semaphore_wait(barrier, n_ctx + n_head - 2)
-
-    def send_state(k, _):
-        to = partner(k)
-        pltpu.make_async_remote_copy(
-            src_ref=meta_out.at[to // per_head],
-            dst_ref=meta_in.at[me],
-            send_sem=sems.at[6],
-            recv_sem=sems.at[7],
-            device_id={"ctx": to},
-        ).start()
-        pltpu.make_async_remote_copy(
-            src_ref=s_out.at[to],
-            dst_ref=s_in_buf.at[me],
-            send_sem=sems.at[10],
-            recv_sem=sems.at[11],
-            device_id={"ctx": to},
-        ).start()
-        return 0
-
-    lax.fori_loop(1, n_ctx, send_state, 0)
+        if h == 0:
+            pl.semaphore_wait(barrier, n_ctx + n_head - 2)
+        lax.fori_loop(1, n_ctx, functools.partial(send_state, h), 0)
+
     meta_in[me] = meta_out[me // per_head]
     s_in_buf[me] = s_out[me]
 

time: 48.3 us -> 49.4 us (1.023)
  Pallas kernels: 47.1 us -> 48.6 us
    pallas_call x1, Pallas kernels: 44.9 us -> 46.5 us  [shards(): pl.pallas_call(functools.partial(kernel, n_ctx, n_head), out_shape=result...]
where the time goes in v6:
time: 49.4 us; the launch traced here: 49.2 us
  Pallas kernels  48.6 us (98%)
  between operations  0.64 us (1%)
    pallas_call x1, Pallas kernels, shards(): pl.pallas_call(functools.partial(kernel, n_ctx, n_head), out_shape=result...  46.5 us
    pallas_call x1, Pallas kernels, shards(): pl.pallas_call(functools.partial(finish, pieces), out_shape=[jax.ShapeDty...  2.15 us

profile of v6, /device:TPU:1, one launch (start us, length us, event | category | flops | bytes accessed | tf_op | source)
XLA Modules:
  0.0 49.2 jit_solution(8636788214388692022)
XLA Ops:
  0.6 46.5 %loglinear_backward.1 = (f32[128,128]{1,0:T(8,128)}, f32[128,128]{1,0:T(8,128)}, f32[1024,256]{1,0:T(8,128)}, f32[2,1024]{1,0:T(2,128)}, f32[10,2,1024]{2,1,0:T(2,128)}) custom-call(bf16[1024,128]{1,0:T(8,128)(2,1)} %q_in.1, bf16[1024,128]{1,0:T(8,128)(2,1)} %k_in.1, bf16[1024,256]{1,0:T(8,128)(2,1)} %v_in.1, bf16[1024,256]{1,0:T(8,128)(2,1)} %c_in.1, ...), custom_call_target="tpu_custom_call" | custom-call | tf_op jit(solution)/shard_map/loglinear_backward/pallas_call | solution.py:751
  47.1 2.2 %store_results.1 = (f32[128,128]{1,0:T(8,128)}, f32[128,128]{1,0:T(8,128)}, f32[1024,256]{1,0:T(8,128)}, f32[2,1024]{1,0:T(2,128)}, f32[10,2,1024]{2,1,0:T(2,128)}) custom-call(f32[128,128]{1,0:T(8,128)} %get-tuple-element.15.refs_0_, f32[128,128]{1,0:T(8,128)} %get-tuple-element.16.refs_1_, f32[1024,256]{1,0:T(8,128)} %get-tuple-element.17.refs_2_, ...), custom_call_target="tpu_custom_call" | custom-call | tf_op jit(solution)/shard_map/store_results/pallas_call | solution.py:795
